TPU v7x, 32 devices: a whole 2x2x4 slice. The times are simulated.
32 devices in a mesh: section: 2 (over core), seq: 4 (over z), wt: 4 (over y, x).
Axes of the slice: x: 2, y: 2, z: 4, core: 2. Of those that a mesh axis runs over, the one named last changes fastest.
Arguments:
- tokens: bfloat16 [2, 4, 1024, 1024], P(None, 'wt', 'seq'), may hold values from -6 to 6
- cotangent: bfloat16 [2, 4, 1024, 1024], P(None, 'wt', 'seq'), may hold values from -6 to 6
- in_weight: bfloat16 [2, 1024, 4384], P('section', 'wt'), may hold values from -0.1875 to 0.1875
- out_weight: bfloat16 [2, 2048, 1024], P('section', 'wt'), may hold values from -0.125 to 0.125
- conv_weight: bfloat16 [2, 4, 2304], P('section', None, 'wt'), may hold values from -3 to 3
- conv_bias: bfloat16 [2, 2304], P('section', 'wt'), may hold values from -0.5 to 0.5
- a_log: bfloat16 [2, 32], P('section', 'wt'), may hold values from -6 to 0
- dt_bias: bfloat16 [2, 32], P('section', 'wt'), may hold values from -4 to -1
- d_skip: bfloat16 [2, 32], P('section', 'wt'), may hold values from 0.5 to 1.5
- gain_in: bfloat16 [2, 1024], P('section', 'wt'), may hold values from 0.5 to 1.5
- gain_out: bfloat16 [2, 2048], P('section', 'wt'), may hold values from 0.5 to 1.5
Outputs:
- states: bfloat16 [2, 2, 4, 1024, 1024], P('section', None, 'wt', 'seq')
- input_grads: bfloat16 [2, 2, 4, 1024, 1024], P('section', None, 'wt', 'seq')
- grad_in_weight: float32 [2, 1024, 4384], P('section', 'wt')
- grad_out_weight: float32 [2, 2048, 1024], P('section', 'wt')
- grad_conv_weight: float32 [2, 4, 2304], P('section', None, 'wt')
- grad_conv_bias: float32 [2, 2304], P('section', 'wt')
- grad_a_log: float32 [2, 32], P('section', 'wt')
- grad_dt_bias: float32 [2, 32], P('section', 'wt')
- grad_d_skip: float32 [2, 32], P('section', 'wt')
- grad_gain_in: float32 [2, 1024], P('section', 'wt')
- grad_gain_out: float32 [2, 2048], P('section', 'wt')
All inputs are finite; a program needn't handle non-finite values.
Results may differ from a plain program's by a relative error of at most 0.019.
Values may be sent and summed in bfloat16 or wider, within the bound.
A program may use at most 448 MiB of HBM per device.

v0:
```python
from functools import partial

import jax
import jax.numpy as jnp
from jax import lax
from jax.sharding import PartitionSpec as P

BLOCK = 256


EPSILON = 1e-05
HIGH = lax.Precision.HIGHEST


def for_sending(array):

    def short(part):
        return part.astype(jnp.bfloat16) if part.dtype == jnp.float32 else part

    return jax.tree.map(short, array)


def shifted(block, axis, distance):
    devices = range(lax.axis_size(axis))
    route = [(i - distance, i) for i in devices if i - distance in devices]
    return lax.ppermute(block, axis, route)


def rms_scale(values, gain):
    return values * lax.rsqrt(jnp.mean(values * values, axis=-1, keepdims=True) + EPSILON) * gain


def causal_conv(inputs, kernel, offset_bias):
    taps_count = kernel.shape[0]
    length = inputs.shape[-2]
    padding = [(0, 0)] * (inputs.ndim - 2) + [(taps_count - 1, 0), (0, 0)]
    padded = jnp.pad(inputs, padding)
    accumulated = offset_bias
    for offset in range(taps_count):
        accumulated = accumulated + kernel[offset] * padded[..., offset : offset + length, :]
    return jax.nn.silu(accumulated)


def state_space(inputs, deltas, rates, b_rows, c_rows, block):
    length, head_count, head_size = inputs.shape
    blocks = length // block
    logdecay = (deltas * rates).reshape(blocks, block, head_count)
    scaled = (inputs * deltas[..., None]).reshape(blocks, block, head_count, head_size)
    b_blocks = b_rows.reshape(blocks, block, -1)
    c_blocks = c_rows.reshape(blocks, block, -1)
    cumulative = jnp.cumsum(logdecay, axis=1)
    cum_heads = jnp.swapaxes(cumulative, 1, 2)
    gram_matrix = jnp.einsum("kin,kjn->kij", c_blocks, b_blocks, precision=HIGH)
    spread = cum_heads[:, :, :, None] - cum_heads[:, :, None, :]
    causal = (jnp.arange(block)[:, None] >= jnp.arange(block)[None, :])[None, None, :, :]
    weights = jnp.where(causal, jnp.exp(jnp.minimum(spread, 0.0)), 0.0) * gram_matrix[:, None, :, :]
    within = jnp.einsum("khij,kjhp->kihp", weights, scaled, precision=HIGH)
    to_end = jnp.exp(cumulative[:, -1:, :] - cumulative)
    contrib = jnp.einsum("kjn,kjhp->khnp", b_blocks, scaled * to_end[..., None], precision=HIGH)
    totals = cumulative[:, -1, :]

    def advance(state_now, element):
        contrib_k, total_k = element
        return (jnp.exp(total_k)[:, None, None] * state_now + contrib_k, state_now)

    initial = jnp.zeros(contrib.shape[1:], inputs.dtype)
    unused_final, entering = lax.scan(advance, initial, (contrib, totals))
    across = (
        jnp.einsum("kin,khnp->kihp", c_blocks, entering, precision=HIGH)
        * jnp.exp(cumulative)[..., None]
    )
    return (within + across).reshape(length, head_count, head_size)


def head_mixer(
    x_heads, dt_heads, bc_full, conv_weight, conv_bias, a_log, dt_bias, d_skip, seq_id, block
):
    batch_rows, length, channels = x_heads.shape
    local_heads = dt_heads.shape[-1]
    head_size = channels // local_heads
    inner = conv_weight.shape[1] - bc_full.shape[-1]
    state_size = bc_full.shape[-1] // 2
    first_chan = seq_id * channels
    first_head = seq_id * local_heads
    kernel = jnp.concatenate(
        [lax.dynamic_slice_in_dim(conv_weight, first_chan, channels, 1), conv_weight[:, inner:]],
        axis=1,
    )
    offset_bias = jnp.concatenate(
        [lax.dynamic_slice_in_dim(conv_bias, first_chan, channels, 0), conv_bias[inner:]]
    )
    rates = -jnp.exp(lax.dynamic_slice_in_dim(a_log, first_head, local_heads, 0))
    deltas = jax.nn.softplus(
        dt_heads + lax.dynamic_slice_in_dim(dt_bias, first_head, local_heads, 0)
    )
    skipping = lax.dynamic_slice_in_dim(d_skip, first_head, local_heads, 0)
    convolved = causal_conv(jnp.concatenate([x_heads, bc_full], axis=-1), kernel, offset_bias)
    x_conv = convolved[..., :channels].reshape(batch_rows, length, local_heads, head_size)
    b_rows = convolved[..., channels : channels + state_size]
    c_rows = convolved[..., channels + state_size :]
    scanned = jax.vmap(partial(state_space, block=block), in_axes=(0, 0, None, 0, 0))(
        x_conv, deltas, rates, b_rows, c_rows
    )
    mixed = scanned + skipping[:, None] * x_conv
    return mixed.reshape(batch_rows, length, channels)


def post_norm(mixed, gate_part, gain_out):
    return rms_scale(mixed * jax.nn.silu(gate_part), gain_out)


def layer_forward(hidden_b, params, seq_id):
    weight_in, weight_out, conv_weight, conv_bias, a_log, dt_bias, d_skip, gain_in, gain_out = (
        params
    )
    inner = weight_out.shape[0]
    state_size = (conv_weight.shape[1] - inner) // 2
    hidden = hidden_b.astype(jnp.float32)
    normed = rms_scale(hidden, gain_in).astype(jnp.bfloat16)
    project = jnp.dot(normed, weight_in, preferred_element_type=jnp.float32)
    gate_part = project[..., :inner]
    x_part = project[..., inner : 2 * inner].astype(jnp.bfloat16)
    bc_part = project[..., 2 * inner : 2 * inner + 2 * state_size].astype(jnp.bfloat16)
    dt_part = project[..., 2 * inner + 2 * state_size :].astype(jnp.bfloat16)
    x_heads, dt_heads = (
        lax.all_to_all(x_part, "seq", split_axis=2, concat_axis=1, tiled=True),
        lax.all_to_all(dt_part, "seq", split_axis=2, concat_axis=1, tiled=True),
    )
    bc_full = lax.all_gather(bc_part, "seq", axis=1, tiled=True)
    mixed = head_mixer(
        x_heads.astype(jnp.float32),
        dt_heads.astype(jnp.float32),
        bc_full.astype(jnp.float32),
        conv_weight,
        conv_bias,
        a_log,
        dt_bias,
        d_skip,
        seq_id,
        BLOCK,
    )
    mixed_tok = lax.all_to_all(
        mixed.astype(jnp.bfloat16), "seq", split_axis=1, concat_axis=2, tiled=True
    )
    scaled = post_norm(mixed_tok.astype(jnp.float32), gate_part, gain_out).astype(jnp.bfloat16)
    output = hidden + jnp.dot(scaled, weight_out, preferred_element_type=jnp.float32)
    return (output, (hidden_b, gate_part, x_heads, dt_heads, bc_full, mixed_tok))


def layer_backward(upstream, saved, params, seq_id):
    weight_in, weight_out, conv_weight, conv_bias, a_log, dt_bias, d_skip, gain_in, gain_out = (
        params
    )
    hidden_b, gate_part, x_heads, dt_heads, bc_full, mixed_tok = saved
    hidden = hidden_b.astype(jnp.float32)
    grad_branch = upstream.astype(jnp.bfloat16)
    scaled_val, post_pull = jax.vjp(post_norm, mixed_tok.astype(jnp.float32), gate_part, gain_out)
    scaled = scaled_val.astype(jnp.bfloat16)
    grad_weight_out = jnp.einsum(
        "bti,btd->id", scaled, grad_branch, preferred_element_type=jnp.float32
    )
    grad_scaled = jnp.einsum(
        "btd,id->bti", grad_branch, weight_out, preferred_element_type=jnp.float32
    )
    grad_mixed, grad_gate, grad_gain_out = post_pull(grad_scaled)
    grad_heads = lax.all_to_all(
        grad_mixed.astype(jnp.bfloat16), "seq", split_axis=2, concat_axis=1, tiled=True
    )
    head_function = partial(head_mixer, seq_id=seq_id, block=BLOCK)
    unused_value, head_pull = jax.vjp(
        head_function,
        x_heads.astype(jnp.float32),
        dt_heads.astype(jnp.float32),
        bc_full.astype(jnp.float32),
        conv_weight,
        conv_bias,
        a_log,
        dt_bias,
        d_skip,
    )
    (
        grad_x,
        grad_dt,
        grad_bc,
        grad_conv_weight,
        grad_conv_bias,
        grad_a_log,
        grad_dt_bias,
        grad_d_skip,
    ) = head_pull(grad_heads.astype(jnp.float32))
    grad_x_tok, grad_dt_tok = (
        lax.all_to_all(grad_x.astype(jnp.bfloat16), "seq", split_axis=1, concat_axis=2, tiled=True),
        lax.all_to_all(
            grad_dt.astype(jnp.bfloat16), "seq", split_axis=1, concat_axis=2, tiled=True
        ),
    )
    grad_bc_tok = jax.tree.map(
        lambda part: part.astype(jnp.float32),
        lax.psum_scatter(for_sending(grad_bc), "seq", scatter_dimension=1, tiled=True),
    ).astype(jnp.bfloat16)
    grad_project = jnp.concatenate(
        [grad_gate.astype(jnp.bfloat16), grad_x_tok, grad_bc_tok, grad_dt_tok], axis=-1
    )
    normed_val, norm_pull = jax.vjp(rms_scale, hidden, gain_in)
    normed = normed_val.astype(jnp.bfloat16)
    grad_weight_in = jnp.einsum(
        "btc,bte->ce", normed, grad_project, preferred_element_type=jnp.float32
    )
    grad_normed = jnp.einsum(
        "bte,ce->btc", grad_project, weight_in, preferred_element_type=jnp.float32
    )
    grad_hidden, grad_gain_in = norm_pull(grad_normed)
    grads = (
        grad_weight_in,
        grad_weight_out,
        grad_conv_weight,
        grad_conv_bias,
        grad_a_log,
        grad_dt_bias,
        grad_d_skip,
        grad_gain_in,
        grad_gain_out,
    )
    return (upstream + grad_hidden, grads)


def local(
    tokens,
    cotangent,
    in_weight,
    out_weight,
    conv_weight,
    conv_bias,
    a_log,
    dt_bias,
    d_skip,
    gain_in,
    gain_out,
):
    section_id = lax.axis_index("section")
    seq_id = lax.axis_index("seq")
    wt_id = lax.axis_index("wt")
    wt_count = lax.axis_size("wt")
    gathered = (
        lax.all_gather(in_weight, "wt", axis=1, tiled=True),
        lax.all_gather(out_weight, "wt", axis=1, tiled=True),
        lax.all_gather(conv_weight, "wt", axis=2, tiled=True),
        lax.all_gather(conv_bias, "wt", axis=1, tiled=True),
        lax.all_gather(a_log, "wt", axis=1, tiled=True),
        lax.all_gather(dt_bias, "wt", axis=1, tiled=True),
        lax.all_gather(d_skip, "wt", axis=1, tiled=True),
        lax.all_gather(gain_in, "wt", axis=1, tiled=True),
        lax.all_gather(gain_out, "wt", axis=1, tiled=True),
    )
    params = (gathered[0][0], gathered[1][0]) + tuple(
        (piece[0].astype(jnp.float32) for piece in gathered[2:])
    )
    micro_count = tokens.shape[0]
    empty = jnp.zeros(tokens.shape[1:], jnp.bfloat16)
    at_first = section_id == 0
    received = empty
    records = []
    outputs = []
    for moment in range(micro_count + 1):
        own_input = tokens[moment] if moment < micro_count else empty
        current = jnp.where(at_first, own_input, received)
        result, saved = layer_forward(current, params, seq_id)
        result = result.astype(jnp.bfloat16)
        if moment < micro_count:
            received = shifted(result, "section", 1)
        records.append(saved)
        outputs.append(result)
    states = jnp.stack(
        [jnp.where(at_first, outputs[micro], outputs[micro + 1]) for micro in range(micro_count)]
    )[None]
    returned = empty
    grads_back = []
    totals = None
    for moment in range(micro_count + 1):
        upstream_in = cotangent[moment] if moment < micro_count else empty
        current = jnp.where(at_first, returned, upstream_in).astype(jnp.float32)
        saved = jax.tree.map(
            partial(jnp.where, at_first),
            records[max(moment - 1, 0)],
            records[min(moment + 1, micro_count)],
        )
        grad_hidden, grads = layer_backward(current, saved, params, seq_id)
        grad_rounded = grad_hidden.astype(jnp.bfloat16)
        if moment < micro_count:
            returned = shifted(grad_rounded, "section", -1)
        grads_back.append(grad_rounded)
        totals = grads if totals is None else jax.tree.map(jnp.add, totals, grads)
    input_grads = jnp.stack(
        [
            jnp.where(at_first, grads_back[micro + 1], grads_back[micro])
            for micro in range(micro_count)
        ]
    )[None]
    (
        grad_win,
        grad_wout,
        grad_convw,
        grad_convb,
        grad_alog,
        grad_dtb,
        grad_skip,
        grad_gin,
        grad_gout,
    ) = totals
    head_total = lax.psum((grad_alog, grad_dtb, grad_skip), ("seq", "wt"))
    head_share = grad_alog.shape[0] // wt_count
    head_parts = tuple(
        (
            lax.dynamic_slice_in_dim(member, wt_id * head_share, head_share, 0)[None]
            for member in head_total
        )
    )
    shares = (
        lax.psum_scatter(
            grad_win.astype(jnp.bfloat16), "wt", scatter_dimension=0, tiled=True
        ).astype(jnp.float32),
        lax.psum_scatter(
            grad_wout.astype(jnp.bfloat16), "wt", scatter_dimension=0, tiled=True
        ).astype(jnp.float32),
        lax.psum_scatter(
            grad_convw.astype(jnp.bfloat16), "wt", scatter_dimension=1, tiled=True
        ).astype(jnp.float32),
        lax.psum_scatter(
            grad_convb.astype(jnp.bfloat16), "wt", scatter_dimension=0, tiled=True
        ).astype(jnp.float32),
        lax.psum_scatter(
            grad_gin.astype(jnp.bfloat16), "wt", scatter_dimension=0, tiled=True
        ).astype(jnp.float32),
        lax.psum_scatter(
            grad_gout.astype(jnp.bfloat16), "wt", scatter_dimension=0, tiled=True
        ).astype(jnp.float32),
    )
    summed = (
        lax.psum(shares[0].astype(jnp.bfloat16), "seq").astype(jnp.float32),
        lax.psum(shares[1].astype(jnp.bfloat16), "seq").astype(jnp.float32),
        lax.psum(shares[2].astype(jnp.bfloat16), "seq").astype(jnp.float32),
        lax.psum(shares[3].astype(jnp.bfloat16), "seq").astype(jnp.float32),
        lax.psum(shares[4].astype(jnp.bfloat16), "seq").astype(jnp.float32),
        lax.psum(shares[5].astype(jnp.bfloat16), "seq").astype(jnp.float32),
    )
    return (
        states,
        input_grads,
        summed[0][None],
        summed[1][None],
        summed[2][None],
        summed[3][None],
        head_parts[0],
        head_parts[1],
        head_parts[2],
        summed[4][None],
        summed[5][None],
    )


def solution(mesh):
    placed = (
        P(None, "wt", "seq", None),
        P(None, "wt", "seq", None),
        P("section", "wt", None),
        P("section", "wt", None),
        P("section", None, "wt"),
        P("section", "wt"),
        P("section", "wt"),
        P("section", "wt"),
        P("section", "wt"),
        P("section", "wt"),
        P("section", "wt"),
    )
    return jax.shard_map(
        local,
        mesh=mesh,
        in_specs=placed,
        out_specs=(
            P("section", None, "wt", "seq", None),
            P("section", None, "wt", "seq", None),
            P("section", "wt", None),
            P("section", "wt", None),
            P("section", None, "wt"),
            P("section", "wt"),
            P("section", "wt"),
            P("section", "wt"),
            P("section", "wt"),
            P("section", "wt"),
            P("section", "wt"),
        ),
        check_vma=False,
    )
```

profile of v0, /device:TPU:0, one launch (start us, length us, event | category | flops | bytes accessed | tf_op | source)
XLA Modules:
  0.0 1968.0 jit_solution(3012567354676598378)
XLA Ops:
  32.7 24.3 %all_gather.37 = bf16[1,4,2304]{1,0,2:T(2,128)(2,1)S(1)} all-gather(bf16[1,4,576]{1,0,2:T(2,128)(2,1)S(1)} %copy.1035), channel_id=1, replica_groups=mesh['section'=2,'seq'=4,'wt'=4] {'wt'}, dimensions={2}, use_global_device_ids=true | all-gather | bytes 23040 | tf_op jit(solution)/shard_map/all_gather | solution.py:247
  58.7 56.0 %all-gather.3.cloned.1.call-done = bf16[1,1024,4384]{1,2,0:T(8,128)(2,1)} async-done(((bf16[1,256,4384]{1,2,0:T(8,128)(2,1)}), bf16[1,1024,4384]{1,2,0:T(8,128)(2,1)}) %all-gather.3.cloned.1.call-update) | async-done | bytes 8978448 | tf_op jit(solution)/shard_map/all_gather | solution.py:245
  130.9 15.7 all_gather.40
  148.1 11.7 copy.1460
  159.8 11.6 reduce.144
  186.4 18.2 all-to-all-done
  288.0 16.5 all-to-all-done.2
  334.9 16.3 all_gather.46
  351.3 11.7 copy.1459
  363.0 11.6 reduce.147
  389.0 18.2 all-to-all-done.3
  481.1 27.1 %all_to_all.234 = bf16[4,2,65536]{2,1,0:T(2,128)(2,1)S(1)} all-to-all(bf16[4,2,65536]{2,1,0:T(2,128)(2,1)S(1)} %reshape.4031), channel_id=1, replica_groups=mesh['section'=2,'seq'=4,'wt'=4] {'seq'}, dimensions={0} | all-to-all | bytes 2097152 | tf_op jit(solution)/shard_map/all_to_all | solution.py:142
  537.6 16.3 all_gather.47
  557.6 11.7 copy.1458
  569.4 11.6 reduce.150
  593.1 20.2 %all-to-all-done.6 = bf16[4,2,65536]{2,1,0:T(2,128)(2,1)} async-done(((bf16[4,2,65536]{2,1,0:T(2,128)(2,1)}), bf16[4,2,65536]{2,1,0:T(2,128)(2,1)}, u32[]{:S(2)}, u32[]{:S(2)}) %all-to-all-start.6) | async-done | bytes 1048608 | tf_op jit(solution)/shard_map/all_to_all | solution.py:126
  641.6 29.0 %fusion.156 = (f32[1,1024,768]{1,2,0:T(8,128)}, f32[1,1024,768]{1,2,0:T(8,128)}, f32[1,1024,768]{1,2,0:T(8,128)}, f32[1,1024,768]{1,2,0:T(8,128)}, f32[1,1024,76...) fusion(f32[1,1024,768]{1,2,0:T(8,128)S(1)} %pad_maximum_fusion.5, f32[768]{0:T(1024)S(1)} %get-tuple-element.1464, ...), kind=kLoop, calls=%fused_computation.255 | loop fusion | flops 37748736 | bytes 34618368 | tf_op jit(solution)/shard_map/jvp(jit(silu))/mul | solution.py:41
  740.2 21.8 %all-to-all-done.8 = bf16[4,2,65536]{2,1,0:T(2,128)(2,1)} async-done(((bf16[4,2,65536]{2,1,0:T(2,128)(2,1)}), bf16[4,2,65536]{2,1,0:T(2,128)(2,1)}, u32[]{:S(2)}, u32[]{:S(2)}) %all-to-all-start.8) | async-done | bytes 1048608 | tf_op jit(solution)/shard_map/all_to_all | solution.py:142
  803.7 11.7 copy.1457
  815.4 11.6 reduce.153
  841.2 19.1 all-to-all-done.9
  877.5 21.9 %while.150 = (s32[]{:T(128)}, f32[1,8,128,64]{3,2,1,0:T(8,128)}, f32[4,1,8,128,64]{4,3,2,1,0:T(8,128)S(1)}, f32[4,1,8]{2,1,0:T(1,128)S(1)}, f32[4,1,8,1,1]{2,4,3...) while((s32[]{:T(128)}, f32[1,8,128,64]{3,2,1,0:T(8,128)}, ...), condition=%wide.region_23.25_spmd.clone, body=%wide.region_22.24_spmd.clone.sunk | while | flops 262147 | bytes 3411212 | solution.py:67
  901.5 11.0 fusion.275
  932.0 16.5 while.151
  1047.0 28.4 %all-to-all-done.10 = bf16[4,2,65536]{2,1,0:T(2,128)(2,1)} async-done(((bf16[4,2,65536]{2,1,0:T(2,128)(2,1)}), bf16[4,2,65536]{2,1,0:T(2,128)(2,1)}, u32[]{:S(2)}, u32[]{:S(2)}) %all-to-all-start.10) | async-done | bytes 1048608 | tf_op jit(solution)/shard_map/all_to_all | solution.py:192
  1103.5 11.7 copy.1456
  1115.2 11.6 reduce.156
  1140.5 21.3 %all-to-all-done.12 = bf16[4,2,65536]{2,1,0:T(2,128)(2,1)} async-done(((bf16[4,2,65536]{2,1,0:T(2,128)(2,1)}), bf16[4,2,65536]{2,1,0:T(2,128)(2,1)}, u32[]{:S(2)}, u32[]{:S(2)}) %all-to-all-start.12) | async-done | bytes 1048608 | tf_op jit(solution)/shard_map/all_to_all | solution.py:166
  1180.7 20.0 %while.152 = (s32[]{:T(128)}, f32[1,8,128,64]{3,2,1,0:T(8,128)}, f32[4,1,8,128,64]{4,3,2,1,0:T(8,128)S(1)}, f32[4,1,8]{2,1,0:T(1,128)}, f32[4,1,8,1,1]{2,4,3,1,0...) while((s32[]{:T(128)}, f32[1,8,128,64]{3,2,1,0:T(8,128)}, ...), condition=%wide.region_44.46_spmd.clone, body=%wide.region_43.45_spmd.clone.sunk | while | flops 262147 | bytes 3411720 | solution.py:67
  1214.7 14.5 while.153
  1236.1 10.2 fusion.273
  1261.9 10.4 reduce-window.80
  1350.0 27.0 %all-to-all-done.13 = bf16[4,2,65536]{2,1,0:T(2,128)(2,1)} async-done(((bf16[4,2,65536]{2,1,0:T(2,128)(2,1)}), bf16[4,2,65536]{2,1,0:T(2,128)(2,1)}, u32[]{:S(2)}, u32[]{:S(2)}) %all-to-all-start.13) | async-done | bytes 1048608 | tf_op jit(solution)/shard_map/all_to_all | solution.py:192
  1409.0 11.6 copy.1455
  1420.7 11.6 reduce.159
  1455.1 11.9 all-to-all-done.15
  1485.9 20.2 %while.154 = (s32[]{:T(128)}, f32[1,8,128,64]{3,2,1,0:T(8,128)}, f32[4,1,8,128,64]{4,3,2,1,0:T(8,128)S(1)}, f32[4,1,8]{2,1,0:T(1,128)}, f32[4,1,8,1,1]{2,4,3,1,0...) while((s32[]{:T(128)}, f32[1,8,128,64]{3,2,1,0:T(8,128)}, ...), condition=%wide.region_65.67_spmd.clone, body=%wide.region_64.66_spmd.clone.sunk | while | flops 262147 | bytes 3411720 | solution.py:67
  1520.2 14.5 while.155
  1541.5 10.2 fusion.271
  1567.2 10.1 reduce-window.86
  1654.0 14.3 fusion.452
  1668.3 13.8 fusion.455
  1688.6 16.4 add_convert_fusion
  1719.1 78.1 %reduce-scatter.15.cloned.1.call-done = bf16[256,4384]{0,1:T(8,128)(2,1)} async-done(((bf16[1024,4384]{0,1:T(8,128)(2,1)}), bf16[256,4384]{0,1:T(8,128)(2,1)}) %reduce-scatter.15.cloned.1.call-update) | async-done | bytes 2244624 | tf_op jit(solution)/shard_map/reduce_scatter | solution.py:319
  1797.8 41.0 %all-reduce.58 = (f32[32]{0:T(128)S(1)}, f32[32]{0:T(128)S(1)}, f32[32]{0:T(128)S(1)}) all-reduce(f32[32]{0:T(128)S(1)} %add_dynamic-update-slice_fusion.4, f32[32]{0:T(128)S(1)} %add_dynamic-update-slice_fusion.2, f32[32]{0:T(128)S(1)} %get-tuple-element.1788), channel_id=1, replica_groups=mesh['section'=2,'seq'=4,'wt'=4] {'seq','wt'}, use_global_device_ids=true, to_apply=%region_107.109 | all-reduce | flops 96 | bytes 768 | tf_op jit(solution)/shard_map/psum | solution.py:310
  1849.2 13.9 all-reduce.59
  1863.3 17.0 all-reduce.61
  1885.4 70.1 %all-reduce.65.cloned.1.call-done = (bf16[1,256,4384]{1,2,0:T(8,128)(2,1)}, bf16[1,512,1024]{2,1,0:T(8,128)(2,1)}) async-done(((bf16[1,256,4384]{1,2,0:T(8,128)(2,1)}, bf16[1,512,1024]{2,1,0:T(8,128)(2,1)}), (bf16[1,256,4384]{1,2,0:T(8,128)(2,1)}, bf16[1,512,1024]{2,1,0:T(8,128)(2,1)})) %all-reduce.65.cloned.1.call-update) | async-done | bytes 3293200 | tf_op jit(solution)/shard_map/psum | solution.py:339
  (1496 shorter events, 1127.1 us)
Async XLA Ops:
  7.3 107.4 %all-gather.3.cloned.1.call-start = ((), (), s32[]{:S(2)}) async-start(), calls=%async_computation.24 | async-start | bytes 11223040 | tf_op jit(solution)/shard_map/all_gather | solution.py:245
  8.0 304.7 %all-gather.5.cloned.1.call-start = ((), (), s32[]{:S(2)}) async-start(), calls=%async_computation.25 | async-start | bytes 5242880 | tf_op jit(solution)/shard_map/all_gather | solution.py:246
  19.2 504.0 %copy-start.137 = (f32[1,1024]{1,0:T(1,128)}, f32[1,1024]{1,0:T(1,128)S(1)}, u32[]{:S(2)}) copy-start(f32[1,1024]{1,0:T(1,128)S(1)} %convert_element_type.971) | copy-start | bytes 12292
  31.8 152.9 %copy-start.221 = (f32[8]{0:T(128)}, f32[8]{0:T(128)S(1)}, u32[]{:S(2)}) copy-start(f32[8]{0:T(128)S(1)} %dynamic-slice.22) | copy-start | bytes 100
  32.4 149.5 %copy-start.229 = (f32[8]{0:T(128)}, f32[8]{0:T(128)S(1)}, u32[]{:S(2)}) copy-start(f32[8]{0:T(128)S(1)} %get-tuple-element.1659) | copy-start | bytes 100
  58.6 657.1 %copy-start.196 = (f32[512]{0:T(512)}, f32[512]{0:T(512)S(1)}, u32[]{:S(2)}) copy-start(f32[512]{0:T(512)S(1)} %mul.2003) | copy-start | bytes 6148
  58.6 155.2 %copy-start.210 = (f32[768]{0:T(1024)}, f32[768]{0:T(1024)S(1)}, u32[]{:S(2)}) copy-start(f32[768]{0:T(1024)S(1)} %pad_maximum_fusion.6) | copy-start | bytes 9220
  58.7 582.4 %copy-start.177 = (f32[768]{0:T(1024)}, f32[768]{0:T(1024)S(1)}, u32[]{:S(2)}) copy-start(f32[768]{0:T(1024)S(1)} %get-tuple-element.1463) | copy-start | bytes 9220
  58.7 582.4 %copy-start.181 = (f32[768]{0:T(1024)}, f32[768]{0:T(1024)S(1)}, u32[]{:S(2)}) copy-start(f32[768]{0:T(1024)S(1)} %get-tuple-element.1464) | copy-start | bytes 9220
  58.7 582.4 %copy-start.185 = (f32[768]{0:T(1024)}, f32[768]{0:T(1024)S(1)}, u32[]{:S(2)}) copy-start(f32[768]{0:T(1024)S(1)} %get-tuple-element.1465) | copy-start | bytes 9220
  126.3 49.7 %all-to-all-start.1 = ((bf16[4,2,1024]{2,1,0:T(2,128)(2,1)}), bf16[4,2,1024]{2,1,0:T(2,128)(2,1)S(1)}, u32[]{:S(2)}, u32[]{:S(2)}) async-start(bf16[4,2,1024]{2,1,0:T(2,128)(2,1)} %reshape.4023), calls=%async_computation.1 | async-start | bytes 32768 | tf_op jit(solution)/shard_map/all_to_all | solution.py:127
  176.0 28.7 %all-to-all-start = ((bf16[4,2,65536]{2,1,0:T(2,128)(2,1)}), bf16[4,2,65536]{2,1,0:T(2,128)(2,1)}, u32[]{:S(2)}, u32[]{:S(2)}) async-start(bf16[4,2,65536]{2,1,0:T(2,128)(2,1)} %reshape.4021), calls=%async_computation | async-start | bytes 2097152 | tf_op jit(solution)/shard_map/all_to_all | solution.py:126
  276.4 28.1 %all-to-all-start.2 = ((bf16[4,2,65536]{2,1,0:T(2,128)(2,1)}), bf16[4,2,65536]{2,1,0:T(2,128)(2,1)S(1)}, u32[]{:S(2)}, u32[]{:S(2)}) async-start(bf16[4,2,65536]{2,1,0:T(2,128)(2,1)} %reshape.4025), calls=%async_computation.2 | async-start | bytes 2097152 | tf_op jit(solution)/shard_map/all_to_all | solution.py:142
  317.1 3.0 collective-permute-start
  331.7 47.5 %all-to-all-start.4 = ((bf16[4,2,1024]{2,1,0:T(2,128)(2,1)}), bf16[4,2,1024]{2,1,0:T(2,128)(2,1)S(1)}, u32[]{:S(2)}, u32[]{:S(2)}) async-start(bf16[4,2,1024]{2,1,0:T(2,128)(2,1)} %reshape.4029), calls=%async_computation.4 | async-start | bytes 32768 | tf_op jit(solution)/shard_map/all_to_all | solution.py:127
  379.2 28.0 %all-to-all-start.3 = ((bf16[4,2,65536]{2,1,0:T(2,128)(2,1)}), bf16[4,2,65536]{2,1,0:T(2,128)(2,1)S(1)}, u32[]{:S(2)}, u32[]{:S(2)}) async-start(bf16[4,2,65536]{2,1,0:T(2,128)(2,1)} %reshape.4027), calls=%async_computation.3 | async-start | bytes 2097152 | tf_op jit(solution)/shard_map/all_to_all | solution.py:126
  518.4 2.8 collective-permute-start.1
  534.4 50.0 %all-to-all-start.7 = ((bf16[4,2,1024]{2,1,0:T(2,128)(2,1)}), bf16[4,2,1024]{2,1,0:T(2,128)(2,1)S(1)}, u32[]{:S(2)}, u32[]{:S(2)}) async-start(bf16[4,2,1024]{2,1,0:T(2,128)(2,1)} %reshape.4035), calls=%async_computation.7 | async-start | bytes 32768 | tf_op jit(solution)/shard_map/all_to_all | solution.py:127
  584.4 28.9 %all-to-all-start.6 = ((bf16[4,2,65536]{2,1,0:T(2,128)(2,1)}), bf16[4,2,65536]{2,1,0:T(2,128)(2,1)}, u32[]{:S(2)}, u32[]{:S(2)}) async-start(bf16[4,2,65536]{2,1,0:T(2,128)(2,1)} %reshape.4033), calls=%async_computation.6 | async-start | bytes 2097152 | tf_op jit(solution)/shard_map/all_to_all | solution.py:126
  732.3 29.7 %all-to-all-start.8 = ((bf16[4,2,65536]{2,1,0:T(2,128)(2,1)}), bf16[4,2,65536]{2,1,0:T(2,128)(2,1)}, u32[]{:S(2)}, u32[]{:S(2)}) async-start(bf16[4,2,65536]{2,1,0:T(2,128)(2,1)} %reshape.4037), calls=%async_computation.8 | async-start | bytes 2097152 | tf_op jit(solution)/shard_map/all_to_all | solution.py:142
  737.0 270.5 %copy-start.159 = (f32[1,256,4,8]{1,3,2,0:T(8,128)}, f32[1,256,4,8]{1,3,2,0:T(8,128)S(1)}, u32[]{:S(2)}) copy-start(f32[1,256,4,8]{1,3,2,0:T(8,128)S(1)} %copy.1091) | copy-start | bytes 98308
  830.4 29.9 %all-to-all-start.9 = ((bf16[4,2,65536]{2,1,0:T(2,128)(2,1)}), bf16[4,2,65536]{2,1,0:T(2,128)(2,1)}, u32[]{:S(2)}, u32[]{:S(2)}) async-start(bf16[4,2,65536]{2,1,0:T(2,128)(2,1)} %reshape.4039), calls=%async_computation.9 | async-start | bytes 2097152 | tf_op jit(solution)/shard_map/all_to_all | solution.py:166
  1011.8 25.3 %all-to-all-start.11 = ((bf16[4,2,1024]{2,1,0:T(2,128)(2,1)}), bf16[4,2,1024]{2,1,0:T(2,128)(2,1)S(1)}, u32[]{:S(2)}, u32[]{:S(2)}) async-start(bf16[4,2,1024]{2,1,0:T(2,128)(2,1)} %reshape.4041), calls=%async_computation.12 | async-start | bytes 32768 | tf_op jit(solution)/shard_map/all_to_all | solution.py:193
  1037.1 38.3 %all-to-all-start.10 = ((bf16[4,2,65536]{2,1,0:T(2,128)(2,1)}), bf16[4,2,65536]{2,1,0:T(2,128)(2,1)}, u32[]{:S(2)}, u32[]{:S(2)}) async-start(bf16[4,2,65536]{2,1,0:T(2,128)(2,1)} %reshape.4043), calls=%async_computation.10 | async-start | bytes 2097152 | tf_op jit(solution)/shard_map/all_to_all | solution.py:192
  1042.2 38.7 %reduce-scatter.9.cloned.1.call-start = ((), (), s32[]{:S(2)}) async-start(), calls=%async_computation.26 | async-start | bytes 655360 | tf_op jit(solution)/shard_map/reduce_scatter | solution.py:199
  1045.8 42.5 %copy-start.260 = (f32[256]{0:T(256)}, f32[256]{0:T(256)S(1)}, u32[]{:S(2)}) copy-start(f32[256]{0:T(256)S(1)} %fusion.574) | copy-start | bytes 3076
  1089.5 4.1 collective-permute-start.2
  1130.3 31.5 %all-to-all-start.12 = ((bf16[4,2,65536]{2,1,0:T(2,128)(2,1)}), bf16[4,2,65536]{2,1,0:T(2,128)(2,1)}, u32[]{:S(2)}, u32[]{:S(2)}) async-start(bf16[4,2,65536]{2,1,0:T(2,128)(2,1)} %reshape.4045), calls=%async_computation.13 | async-start | bytes 2097152 | tf_op jit(solution)/shard_map/all_to_all | solution.py:166
  1138.2 37.9 %copy-start.118 = (f32[4,256,128,1]{2,1,3,0:T(8,128)}, f32[4,256,128,1]{2,1,3,0:T(8,128)S(1)}, u32[]{:S(2)}) copy-start(f32[4,256,128,1]{2,1,3,0:T(8,128)S(1)} %copy.1231) | copy-start | bytes 1572868
  1307.3 30.3 %all-to-all-start.14 = ((bf16[4,2,1024]{2,1,0:T(2,128)(2,1)}), bf16[4,2,1024]{2,1,0:T(2,128)(2,1)S(1)}, u32[]{:S(2)}, u32[]{:S(2)}) async-start(bf16[4,2,1024]{2,1,0:T(2,128)(2,1)} %reshape.4047), calls=%async_computation.16 | async-start | bytes 32768 | tf_op jit(solution)/shard_map/all_to_all | solution.py:193
  1337.6 39.4 %all-to-all-start.13 = ((bf16[4,2,65536]{2,1,0:T(2,128)(2,1)}), bf16[4,2,65536]{2,1,0:T(2,128)(2,1)}, u32[]{:S(2)}, u32[]{:S(2)}) async-start(bf16[4,2,65536]{2,1,0:T(2,128)(2,1)} %reshape.4049), calls=%async_computation.14 | async-start | bytes 2097152 | tf_op jit(solution)/shard_map/all_to_all | solution.py:192
  1342.7 39.8 %reduce-scatter.11.cloned.1.call-start = ((), (), s32[]{:S(2)}) async-start(), calls=%async_computation.27 | async-start | bytes 655360 | tf_op jit(solution)/shard_map/reduce_scatter | solution.py:199
  1346.4 43.6 %copy-start.269 = (f32[256]{0:T(256)}, f32[256]{0:T(256)S(1)}, u32[]{:S(2)}) copy-start(f32[256]{0:T(256)S(1)} %fusion.576) | copy-start | bytes 3076
  1391.4 7.7 collective-permute-start.3
  1435.7 31.3 %all-to-all-start.15 = ((bf16[4,2,65536]{2,1,0:T(2,128)(2,1)}), bf16[4,2,65536]{2,1,0:T(2,128)(2,1)}, u32[]{:S(2)}, u32[]{:S(2)}) async-start(bf16[4,2,65536]{2,1,0:T(2,128)(2,1)} %reshape.4051), calls=%async_computation.17 | async-start | bytes 2097152 | tf_op jit(solution)/shard_map/all_to_all | solution.py:166
  1440.0 248.6 %reduce-scatter.13.cloned.1.call-start = ((), (), s32[]{:S(2)}) async-start(), calls=%async_computation.28 | async-start | bytes 655360 | tf_op jit(solution)/shard_map/reduce_scatter | solution.py:199
  1440.7 40.6 %copy-start.173 = (f32[4,256,8]{1,2,0:T(8,128)}, f32[4,256,8]{1,2,0:T(8,128)S(1)}, u32[]{:S(2)}) copy-start(f32[4,256,8]{1,2,0:T(8,128)S(1)} %fusion.532) | copy-start | bytes 98308
  1610.1 109.0 %reduce-scatter.17.cloned.1.call-start = ((), (), s32[]{:S(2)}) async-start(), calls=%async_computation.30 | async-start | bytes 5242880 | tf_op jit(solution)/shard_map/reduce_scatter | solution.py:322
  1624.3 24.5 %all-to-all-start.17 = ((bf16[4,2,1024]{2,1,0:T(2,128)(2,1)}), bf16[4,2,1024]{2,1,0:T(2,128)(2,1)S(1)}, u32[]{:S(2)}, u32[]{:S(2)}) async-start(bf16[4,2,1024]{2,1,0:T(2,128)(2,1)} %reshape.4053), calls=%async_computation.20 | async-start | bytes 32768 | tf_op jit(solution)/shard_map/all_to_all | solution.py:193
  1648.8 34.2 %all-to-all-start.16 = ((bf16[4,2,65536]{2,1,0:T(2,128)(2,1)}), bf16[4,2,65536]{2,1,0:T(2,128)(2,1)}, u32[]{:S(2)}, u32[]{:S(2)}) async-start(bf16[4,2,65536]{2,1,0:T(2,128)(2,1)} %reshape.4055), calls=%async_computation.18 | async-start | bytes 2097152 | tf_op jit(solution)/shard_map/all_to_all | solution.py:192
  1653.9 143.4 %reduce-scatter.15.cloned.1.call-start = ((), (), s32[]{:S(2)}) async-start(), calls=%async_computation.29 | async-start | bytes 11223040 | tf_op jit(solution)/shard_map/reduce_scatter | solution.py:319
  1705.2 135.5 %reduce-scatter.19.cloned.1.call-start = ((), (), s32[]{:S(2)}) async-start(), calls=%async_computation.31 | async-start | bytes 737280
  1718.7 78.6 %copy-start.292 = (f32[8]{0:T(128)S(1)}, f32[8]{0:T(128)}, u32[]{:S(2)}) copy-start(f32[8]{0:T(128)} %get-tuple-element.1728) | copy-start | bytes 100
  1718.7 78.8 %copy-start.289 = (f32[8]{0:T(128)S(1)}, f32[8]{0:T(128)}, u32[]{:S(2)}) copy-start(f32[8]{0:T(128)} %get-tuple-element.1467) | copy-start | bytes 100
  1718.7 79.0 %copy-start.288 = (f32[8]{0:T(128)S(1)}, f32[8]{0:T(128)}, u32[]{:S(2)}) copy-start(f32[8]{0:T(128)} %get-tuple-element.1466) | copy-start | bytes 100
  1718.7 123.1 %copy-start.191 = (bf16[1,256,256]{1,2,0:T(8,128)(2,1)S(1)}, bf16[1,256,256]{1,2,0:T(8,128)(2,1)}, u32[]{:S(2)}) copy-start(bf16[1,256,256]{1,2,0:T(8,128)(2,1)} %reduce-scatter.13.cloned.1.call-done) | copy-start | bytes 393220
  1718.8 236.7 %all-reduce.65.cloned.1.call-start = ((), (), s32[]{:S(2)}) async-start(), calls=%async_computation.32 | async-start | bytes 6586368 | tf_op jit(solution)/shard_map/psum | solution.py:339
  1841.8 40.8 %copy-start.149 = (bf16[1,256,1024]{2,1,0:T(8,128)(2,1)S(1)}, bf16[1,256,1024]{2,1,0:T(8,128)(2,1)}, u32[]{:S(2)}) copy-start(bf16[1,256,1024]{2,1,0:T(8,128)(2,1)} %copy-done.147) | copy-start | bytes 1572868
  (303 other events, 1814.5 us)
Sparse Core Ops, SparseCore 0:
  9.9 104.7 all-gather.2
  116.5 52.6 all-gather.4
  1045.8 27.9 reduce-scatter.8
  1346.4 28.6 reduce-scatter.10
  1610.3 19.9 reduce-scatter.12
  1633.6 51.0 reduce-scatter.16
  1705.3 91.8 reduce-scatter.14
  1801.0 25.1 reduce-scatter.18
  1828.6 126.8 all-reduce.64
where the time goes:
time: 1980 us; the launch traced here: 1970 us
  local copies, waits for them, and re-layouts  471 us (24%)
  other arithmetic  442 us (22%)
  waiting for transfers between devices  411 us (21%)
  matrix products  339 us (17%)
  blocking collectives  199 us (10%)
  starting transfers between devices  80.8 us (4%)
  between operations  22 us (1%)
    unnamed x36, other arithmetic  134 us
    unnamed x648, local copies, waits for them, and re-layouts  109 us
    reduce_scatter x1, waiting for transfers between devices, local(): lax.psum_scatter(grad_win.astype(jnp.bfloat16), 'wt', scatter_dimension=0...  78.1 us
    dot_general x9, matrix products, state_space(): within = jnp.einsum('khij,kjhp->kihp', weights, scaled, precision=HIGH)  75.7 us
    psum x1, waiting for transfers between devices, local(): lax.psum(shares[0].astype(jnp.bfloat16), 'seq').astype(jnp.float32)  70.1 us
    another operation x38, other arithmetic  69.4 us
    all_to_all x3, waiting for transfers between devices, layer_forward(): lax.all_to_all(x_part, 'seq', split_axis=2, concat_axis=1, tiled=True)  56.6 us
    all_gather x1, waiting for transfers between devices, local(): lax.all_gather(in_weight, 'wt', axis=1, tiled=True)  56 us
  transfers between devices with their start and end apart: 30, of which 16 were waited for; matrix products, arithmetic and copies ran while one was open for 21% of the time, Pallas kernels for 0%

commit v1 on v0

v1 whole, which is shorter than its diff:
```python
import jax
import jax.numpy as jnp
from jax import lax
from jax.experimental import pallas as pl
from jax.experimental.pallas import tpu as pltpu
from jax.sharding import PartitionSpec as P

EPSILON = 1e-05
HIGH = lax.Precision.HIGHEST
F32 = jnp.float32
BF16 = jnp.bfloat16
LANES = 128


def shifted(block, axis, distance):
    devices = range(lax.axis_size(axis))
    route = [(i - distance, i) for i in devices if i - distance in devices]
    return lax.ppermute(block, axis, route)


def swapped(block):
    return lax.ppermute(block, "section", [(0, 1), (1, 0)])


def rms_scale(values, gain):
    return values * lax.rsqrt(jnp.mean(values * values, axis=-1, keepdims=True) + EPSILON) * gain


def post_norm(mixed, gate_part, gain_out):
    return rms_scale(mixed * jax.nn.silu(gate_part), gain_out)


def dot(a, b, over):
    return lax.dot_general(
        a.astype(BF16), b.astype(BF16), (over, ((), ())), preferred_element_type=F32
    )


ROWS_COLS = ((1,), (0,))
COLS_COLS = ((1,), (1,))
ROWS_ROWS = ((0,), (0,))


def head_decay(head, cum_ref, cum_t_ref):
    heads = lax.broadcasted_iota(jnp.int32, cum_ref.shape, 1)
    column = jnp.sum(jnp.where(heads == head, cum_ref[...], 0.0), axis=1, keepdims=True)
    row = cum_t_ref[pl.ds(head, 1), :]
    return jnp.exp(jnp.minimum(column - row, 0.0))


def causal_gram(c_ref, b_ref, gram):
    length = gram.shape[0]
    product = dot(c_ref[...], b_ref[...], COLS_COLS)
    rows = lax.broadcasted_iota(jnp.int32, (length, length), 0)
    cols = lax.broadcasted_iota(jnp.int32, (length, length), 1)
    gram[...] = jnp.where(rows >= cols, product, 0.0)


def within_kernel(head_size, u_ref, cum_ref, cum_t_ref, b_ref, c_ref, y_ref, gram):
    tile = pl.program_id(0)
    per_tile = LANES // head_size

    @pl.when(tile == 0)
    def _():
        causal_gram(c_ref, b_ref, gram)

    u = u_ref[...]
    owner = lax.broadcasted_iota(jnp.int32, u.shape, 1) // head_size
    total = jnp.zeros(u.shape, F32)
    for k in range(per_tile):
        weights = head_decay(tile * per_tile + k, cum_ref, cum_t_ref) * gram[...]
        total += dot(weights, jnp.where(owner == k, u, 0.0), ROWS_COLS)
    y_ref[...] = total


def within_back_kernel(
    head_size,
    u_ref,
    dy_ref,
    cum_ref,
    cum_t_ref,
    b_ref,
    c_ref,
    du_ref,
    dgram_ref,
    rows_ref,
    cols_ref,
    gram,
):
    tile = pl.program_id(0)
    per_tile = LANES // head_size

    @pl.when(tile == 0)
    def _():
        causal_gram(c_ref, b_ref, gram)
        dgram_ref[...] = jnp.zeros_like(dgram_ref)
        rows_ref[...] = jnp.zeros_like(rows_ref)

    u = u_ref[...].astype(BF16)
    dy = dy_ref[...]
    length = u.shape[0]
    owner = lax.broadcasted_iota(jnp.int32, dy.shape, 1) // head_size
    heads = lax.broadcasted_iota(jnp.int32, rows_ref.shape, 1)
    causal = lax.broadcasted_iota(jnp.int32, (length, length), 0) >= lax.broadcasted_iota(
        jnp.int32, (length, length), 1
    )
    total = jnp.zeros(dy.shape, F32)
    for k in range(per_tile):
        head = tile * per_tile + k
        decay = head_decay(head, cum_ref, cum_t_ref)
        weights = decay * gram[...]
        dy_own = jnp.where(owner == k, dy, 0.0).astype(BF16)
        dweights = dot(dy_own, u, COLS_COLS)
        dgram_ref[...] += jnp.where(causal, dweights * decay, 0.0)
        pairs = dweights * weights
        rows_ref[...] += jnp.where(heads == head, jnp.sum(pairs, axis=1, keepdims=True), 0.0)
        cols_ref[pl.ds(head, 1), :] = jnp.sum(pairs, axis=0, keepdims=True)
        total += dot(weights, dy_own, ROWS_ROWS)
    du_ref[...] = total


def full(shape):
    return pl.BlockSpec(shape, lambda i: (0,) * len(shape))


def within(u, cum, b, c, head_size):
    length, channels = u.shape
    cum_t = cum.T
    tile = pl.BlockSpec((length, LANES), lambda i: (0, i))
    return pl.pallas_call(
        lambda *refs: within_kernel(head_size, *refs),
        grid=(channels // LANES,),
        out_shape=jax.ShapeDtypeStruct(u.shape, F32),
        in_specs=[tile, full(cum.shape), full(cum_t.shape), full(b.shape), full(c.shape)],
        out_specs=tile,
        scratch_shapes=[pltpu.VMEM((length, length), F32)],
        cost_estimate=pl.CostEstimate(
            flops=length * length * channels * 8,
            bytes_accessed=8 * u.size,
            transcendentals=length * length * channels // head_size,
        ),
    )(u, cum, cum_t, b, c)


def within_back(u, dy, cum, b, c, head_size):
    length, channels = u.shape
    cum_t = cum.T
    tile = pl.BlockSpec((length, LANES), lambda i: (0, i))
    return pl.pallas_call(
        lambda *refs: within_back_kernel(head_size, *refs),
        grid=(channels // LANES,),
        out_shape=(
            jax.ShapeDtypeStruct(u.shape, F32),
            jax.ShapeDtypeStruct((length, length), F32),
            jax.ShapeDtypeStruct(cum.shape, F32),
            jax.ShapeDtypeStruct(cum_t.shape, F32),
        ),
        in_specs=[tile, tile, full(cum.shape), full(cum_t.shape), full(b.shape), full(c.shape)],
        out_specs=(tile, full((length, length)), full(cum.shape), full(cum_t.shape)),
        scratch_shapes=[pltpu.VMEM((length, length), F32)],
        cost_estimate=pl.CostEstimate(
            flops=length * length * channels * 16,
            bytes_accessed=12 * u.size,
            transcendentals=length * length * channels // head_size,
        ),
    )(u, dy, cum, cum_t, b, c)


def carried(term, decay, distance):
    count = lax.axis_size("seq")
    if count == 1:
        return jnp.zeros_like(term)
    state = shifted(term.astype(BF16), "seq", distance).astype(F32)
    for _ in range(count - 2):
        state = shifted((term + decay * state).astype(BF16), "seq", distance).astype(F32)
    return state


def split_halves(array, parts, first):
    share = array.shape[1] // (2 * parts)
    pieces = [array[:, j * share : (j + 1) * share] for j in range(2 * parts)]
    even = jnp.concatenate(pieces[0::2], axis=1)
    odd = jnp.concatenate(pieces[1::2], axis=1)
    return jnp.where(first, even, odd), jnp.where(first, odd, even)


def join_halves(mine, other, parts, first):
    even, odd = jnp.where(first, mine, other), jnp.where(first, other, mine)
    share = mine.shape[1] // parts
    pieces = []
    for j in range(parts):
        pieces += [even[:, j * share : (j + 1) * share], odd[:, j * share : (j + 1) * share]]
    return jnp.concatenate(pieces, axis=1)


def head_map(heads, channels):
    return (jnp.arange(channels)[None, :] // (channels // heads) == jnp.arange(heads)[:, None]).astype(F32)


def layer_forward(hidden_b, weights, small, first, parts):
    (win_mine, win_other), (wout_mine, wout_other) = weights
    conv_weight, conv_bias, a_log, dt_bias, d_skip, gain_in, gain_out = small
    heads, inner, conv = a_log.shape[0], gain_out.shape[0], conv_bias.shape[0]
    head_size = inner // heads
    state_size = (conv - inner) // 2
    taps = conv_weight.shape[0]
    hidden = hidden_b.astype(F32)
    length = hidden.shape[0]
    normed = rms_scale(hidden, gain_in).astype(BF16)
    normed_mine, normed_other = split_halves(normed, parts, first)
    project = dot(normed_mine, win_mine, ROWS_COLS) + dot(normed_other, win_other, ROWS_COLS)
    gate = project[:, :inner]
    v = project[:, inner : inner + conv].astype(BF16)
    dt_raw = project[:, inner + conv :].astype(BF16).astype(F32)
    halo = shifted(v[length - taps + 1 :], "seq", 1)
    padded = jnp.concatenate([halo, v], axis=0).astype(F32)
    pre = conv_bias
    for k in range(taps):
        pre = pre + conv_weight[k] * padded[k : k + length]
    conv_out = jax.nn.silu(pre)
    xs = conv_out[:, :inner]
    b = conv_out[:, inner : inner + state_size]
    c = conv_out[:, inner + state_size :]
    delta = jax.nn.softplus(dt_raw + dt_bias)
    rate = -jnp.exp(a_log)
    tri = jnp.tril(jnp.ones((length, length), F32))
    cum = jnp.dot(tri, delta * rate, precision=HIGH)
    last = cum[length - 1 :]
    widen = head_map(heads, inner)
    delta_w = jnp.dot(delta, widen, precision=HIGH)
    cum_w = jnp.dot(jnp.exp(cum), widen, precision=HIGH)
    end_w = jnp.dot(jnp.exp(last - cum), widen, precision=HIGH)
    decay = cum_w[length - 1 :]
    skip_w = jnp.repeat(d_skip, head_size)
    u = xs * delta_w
    term = dot(b, u * end_w, ROWS_ROWS)
    entering = carried(term, decay, 1)
    inside = within(u, cum, b, c, head_size)
    across = cum_w * dot(c, entering, ROWS_COLS)
    mixed = (inside + across + skip_w * xs).astype(BF16)
    scaled = post_norm(mixed.astype(F32), gate, gain_out).astype(BF16)
    scaled_mine, scaled_other = split_halves(scaled, parts, first)
    output = (
        hidden
        + dot(scaled_mine, wout_mine, ROWS_COLS)
        + dot(scaled_other, wout_other, ROWS_COLS)
    )
    saved = (
        hidden, normed_mine, normed_other, gate, padded, dt_raw, pre, xs, b, c, delta, rate, tri,
        cum, widen, delta_w, cum_w, end_w, decay, skip_w, u, entering, across, mixed,
        scaled_mine, scaled_other,
    )
    return output.astype(BF16), saved


def layer_backward(upstream_b, saved, weights, small, first, parts):
    (win_mine, win_other), (wout_mine, wout_other) = weights
    conv_weight, conv_bias, a_log, dt_bias, d_skip, gain_in, gain_out = small
    (
        hidden, normed_mine, normed_other, gate, padded, dt_raw, pre, xs, b, c, delta, rate, tri,
        cum, widen, delta_w, cum_w, end_w, decay, skip_w, u, entering, across, mixed,
        scaled_mine, scaled_other,
    ) = saved
    heads, inner = a_log.shape[0], gain_out.shape[0]
    head_size = inner // heads
    taps = conv_weight.shape[0]
    length = hidden.shape[0]

    def narrow(array):
        return dot(array, widen, COLS_COLS)

    grad_scaled = join_halves(
        dot(upstream_b, wout_mine, COLS_COLS), dot(upstream_b, wout_other, COLS_COLS), parts, first
    )
    grad_wout = (
        dot(scaled_mine, upstream_b, ROWS_ROWS),
        dot(scaled_other, upstream_b, ROWS_ROWS).astype(BF16),
    )
    _, post_pull = jax.vjp(post_norm, mixed.astype(F32), gate, gain_out)
    grad_mixed, grad_gate, grad_gain_out = post_pull(grad_scaled)
    dy = grad_mixed.astype(BF16).astype(F32)
    dy_cum = dy * cum_w
    a_term = dot(c, dy_cum, ROWS_ROWS)
    a_out = carried(a_term, decay, -1)
    du_inside, dgram, pair_rows, pair_cols = within_back(u, dy, cum, b, c, head_size)
    grad_c = dot(dy_cum, entering, COLS_COLS) + dot(dgram, b, ROWS_COLS)
    grad_b = dot(u * end_w, a_out, COLS_COLS) + dot(dgram, c, ROWS_ROWS)
    du_state = end_w * dot(b, a_out, ROWS_COLS)
    moved = narrow(du_state * u)
    decay_grad = jnp.sum(a_out * entering, axis=0, keepdims=True) * decay
    grad_last = jnp.sum(moved, axis=0, keepdims=True) + jnp.dot(
        decay_grad, widen.T, precision=HIGH
    )
    grad_cum = pair_rows - pair_cols.T + narrow(dy * across) - moved
    grad_log = lax.dot_general(tri, grad_cum, (ROWS_ROWS, ((), ())), precision=HIGH) + grad_last
    du = du_inside + du_state
    grad_xs = du * delta_w + skip_w * dy
    grad_delta = grad_log * rate + narrow(du * xs)
    grad_a_log = jnp.sum(grad_log * delta, axis=0) * rate
    grad_skip = jnp.dot(jnp.sum(dy * xs, axis=0), widen.T, precision=HIGH)
    grad_dt_raw = grad_delta * jax.nn.sigmoid(dt_raw + dt_bias)
    grad_dt_bias = jnp.sum(grad_dt_raw, axis=0)
    sig = jax.nn.sigmoid(pre)
    grad_pre = jnp.concatenate([grad_xs, grad_b, grad_c], axis=1) * sig * (1.0 + pre * (1.0 - sig))
    halo = shifted(grad_pre[: taps - 1].astype(BF16), "seq", -1).astype(F32)
    grad_padded = jnp.concatenate([grad_pre, halo], axis=0)
    grad_v = sum(
        conv_weight[k] * grad_padded[taps - 1 - k : taps - 1 - k + length] for k in range(taps)
    )
    grad_conv_weight = jnp.stack(
        [jnp.sum(grad_pre * padded[k : k + length], axis=0) for k in range(taps)]
    )
    grad_conv_bias = jnp.sum(grad_pre, axis=0)
    grad_project = jnp.concatenate(
        [grad_gate.astype(BF16), grad_v.astype(BF16), grad_dt_raw.astype(BF16)], axis=1
    )
    grad_normed = join_halves(
        dot(grad_project, win_mine, COLS_COLS),
        dot(grad_project, win_other, COLS_COLS),
        parts,
        first,
    )
    grad_win = (
        dot(normed_mine, grad_project, ROWS_ROWS),
        dot(normed_other, grad_project, ROWS_ROWS).astype(BF16),
    )
    _, norm_pull = jax.vjp(rms_scale, hidden, gain_in)
    grad_hidden, grad_gain_in = norm_pull(grad_normed)
    grad_small = (
        grad_conv_weight, grad_conv_bias, grad_a_log, grad_dt_bias, grad_skip, grad_gain_in,
        grad_gain_out,
    )
    return (upstream_b.astype(F32) + grad_hidden).astype(BF16), grad_win, grad_wout, grad_small


def reduced(grad):
    mine, other = grad
    both = (mine + swapped(other).astype(F32)).astype(BF16)
    share = lax.psum_scatter(both, "wt", scatter_dimension=0, tiled=True)
    return lax.psum(share, "seq")


def own_layer(layers, first):
    recv0 = lax.ppermute(layers[0], "section", [(1, 0)])
    recv1 = lax.ppermute(layers[1], "section", [(0, 1)])
    own = jnp.where(first, layers[0], layers[1])
    recv = jnp.where(first, recv0, recv1)
    joined = jnp.concatenate([jnp.where(first, own, recv), jnp.where(first, recv, own)], axis=0)
    return joined.astype(F32)[None]


def by_layer(results, first):
    own = jnp.where(first, results[0], results[1])
    recv = swapped(jnp.where(first, results[1], results[0]))
    return jnp.stack([jnp.where(first, own, recv), jnp.where(first, recv, own)])[None, :, None]


def local(tokens, cotangent, in_weight, out_weight, *small_shards):
    section = lax.axis_index("section")
    first = section == 0
    wt_id = lax.axis_index("wt")
    parts = lax.axis_size("wt")

    def halves(weight):
        rows = weight.shape[1] // 2
        keep = lax.dynamic_slice_in_dim(weight[0], section * rows, rows, 0)
        recv = swapped(lax.dynamic_slice_in_dim(weight[0], (1 - section) * rows, rows, 0))
        return jnp.where(first, keep, recv), jnp.where(first, recv, keep)

    def gathered(half):
        mine = lax.all_gather(half, "wt", axis=0, tiled=True)
        return mine, swapped(mine)

    win_halves, wout_halves = halves(in_weight), halves(out_weight)
    flat = jnp.concatenate([shard[0].reshape(-1) for shard in small_shards])
    packed = lax.all_gather(flat, ("section", "wt"), axis=0, tiled=False)
    packed = packed.reshape(2, parts, -1).astype(F32)
    smalls = []
    for layer in range(2):
        rest, small = packed[layer], []
        for shard in small_shards:
            shape = shard.shape[1:]
            size = shard[0].size
            piece, rest = rest[:, :size], rest[:, size:]
            if len(shape) == 2:
                piece = piece.reshape((parts,) + shape).swapaxes(0, 1)
                small.append(piece.reshape(shape[0], -1))
            else:
                small.append(piece.reshape(-1))
        smalls.append(tuple(small))
    win0 = gathered(win_halves[0])
    wout0 = gathered(wout_halves[0])
    win1 = gathered(win_halves[1])
    wout1 = gathered(wout_halves[1])
    weights = ((win0, wout0), (win1, wout1))

    own_tokens = lax.dynamic_index_in_dim(tokens, section, 0, keepdims=False)[0]
    own_cotangent = lax.dynamic_index_in_dim(cotangent, section, 0, keepdims=False)[0]
    out0, saved0 = layer_forward(own_tokens, weights[0], smalls[0], first, parts)
    out1, saved1 = layer_forward(out0, weights[1], smalls[1], first, parts)
    states = by_layer((out0, out1), first)
    back1, gwin1, gwout1, gsmall1 = layer_backward(
        own_cotangent, saved1, weights[1], smalls[1], first, parts
    )
    sum_wout1, sum_win1 = reduced(gwout1), reduced(gwin1)
    back0, gwin0, gwout0, gsmall0 = layer_backward(
        back1, saved0, weights[0], smalls[0], first, parts
    )
    sum_wout0, sum_win0 = reduced(gwout0), reduced(gwin0)
    input_grads = by_layer((back0, back1), first)

    flat0 = jnp.concatenate([g.reshape(-1) for g in gsmall0])
    flat1 = jnp.concatenate([g.reshape(-1) for g in gsmall1])
    total = jnp.where(first, flat0, flat1) + swapped(jnp.where(first, flat1, flat0))
    total = lax.psum(total, ("seq", "wt"))
    small_out, at = [], 0
    for g in gsmall0:
        piece = total[at : at + g.size].reshape(g.shape)
        at += g.size
        axis = g.ndim - 1
        share = g.shape[axis] // parts
        small_out.append(lax.dynamic_slice_in_dim(piece, wt_id * share, share, axis)[None])
    return (
        states,
        input_grads,
        own_layer((sum_win0, sum_win1), first),
        own_layer((sum_wout0, sum_wout1), first),
        *small_out,
    )


def solution(mesh):
    shards = (
        P("section", "wt", None),
        P("section", "wt", None),
        P("section", None, "wt"),
        P("section", "wt"),
        P("section", "wt"),
        P("section", "wt"),
        P("section", "wt"),
        P("section", "wt"),
        P("section", "wt"),
    )
    return jax.shard_map(
        local,
        mesh=mesh,
        in_specs=(P(None, "wt", "seq", None), P(None, "wt", "seq", None)) + shards,
        out_specs=(P("section", None, "wt", "seq", None), P("section", None, "wt", "seq", None))
        + shards,
        check_vma=False,
    )
```

time: 1980 us -> 864 us (0.44)
  local copies, waits for them, and re-layouts: 471 us -> 61.6 us
  other arithmetic: 442 us -> 61.3 us
  matrix products: 339 us -> 120 us
  blocking collectives: 199 us -> 108 us
  Pallas kernels: 0 us -> 52.4 us
  waiting for transfers between devices: 411 us -> 376 us
  starting transfers between devices: 80.8 us -> 54.9 us
    all_to_all x17 -> x0, waiting for transfers between devices: 203 us -> none  [the longest x3 56.6 us: layer_forward(): lax.all_to_all(x_part, 'seq', split_axis=2, concat_axis=1, tiled=True)]
    dot_general x57 -> x60, matrix products: 320 us -> 120 us  [the longest x46 100 us: dot(): lax.dot_general(a.astype(BF16), b.astype(BF16), (over, ((), ())), preferr...]
    unnamed x36 -> x9, other arithmetic: 134 us -> 2.19 us
    convert_element_type x34 -> x1, local copies, waits for them, and re-layouts: 100 us -> 0.12 us  [local(): packed = packed.reshape(2, parts, -1).astype(F32)]
    all_gather x6 -> x0, blocking collectives: 90.1 us -> none  [the longest x3 48.2 us: layer_forward(): bc_full = lax.all_gather(bc_part, 'seq', axis=1, tiled=True)]
    all_to_all x17 -> x0, starting transfers between devices: 74.3 us -> none  [the longest x3 16.3 us: layer_forward(): lax.all_to_all(x_part, 'seq', split_axis=2, concat_axis=1, tiled=True)]
    another operation x41 -> x4, other arithmetic: 74.4 us -> 1.41 us  [the longest x2 1.33 us: by_layer(): jnp.stack([jnp.where(first, own, recv), jnp.where(first, recv, own)])]
    unnamed x648 -> x495, local copies, waits for them, and re-layouts: 109 us -> 39.7 us
  transfers between devices with their start and end apart: 30 -> 42, of which waited for: 16 -> 20; matrix products, arithmetic and copies ran while one was open for 21% -> 18% of each run, Pallas kernels for 0% -> 6%
where the time goes in v1:
time: 864 us; the launch traced here: 853 us
  waiting for transfers between devices  376 us (44%)
  matrix products  120 us (14%)
  blocking collectives  108 us (12%)
  local copies, waits for them, and re-layouts  61.6 us (7%)
  other arithmetic  61.3 us (7%)
  starting transfers between devices  54.9 us (6%)
  Pallas kernels  52.4 us (6%)
  between operations  18.7 us (2%)
    all_gather x4, waiting for transfers between devices, gathered(): mine = lax.all_gather(half, 'wt', axis=0, tiled=True)  121 us
    dot_general x46, matrix products, dot(): lax.dot_general(a.astype(BF16), b.astype(BF16), (over, ((), ())), preferr...  100 us
    psum x1, blocking collectives, local(): total = lax.psum(total, ('seq', 'wt'))  79.4 us
    reduce_scatter x2, waiting for transfers between devices, reduced(): share = lax.psum_scatter(both, 'wt', scatter_dimension=0, tiled=True)  75.4 us
    ppermute x16, waiting for transfers between devices, shifted(): return lax.ppermute(block, axis, route)  69.5 us
    unnamed x11, waiting for transfers between devices  45.7 us
    psum x1, waiting for transfers between devices, reduced(): return lax.psum(share, 'seq')  43.1 us
    ppermute x16, starting transfers between devices, shifted(): return lax.ppermute(block, axis, route)  43.1 us
  transfers between devices with their start and end apart: 42, of which 20 were waited for; matrix products, arithmetic and copies ran while one was open for 18% of the time, Pallas kernels for 6%

profile of v1, /device:TPU:0, one launch (start us, length us, event | category | flops | bytes accessed | tf_op | source)
XLA Modules:
  0.0 853.1 jit_solution(12940763199179722726)
XLA Ops:
  19.2 53.6 %all-gather.6.cloned.1.call-done = bf16[512,4384]{0,1:T(8,128)(2,1)} async-done(((bf16[128,4384]{0,1:T(8,128)(2,1)}), bf16[512,4384]{0,1:T(8,128)(2,1)}) %all-gather.6.cloned.1.call-update) | async-done | bytes 4489232 | tf_op jit(solution)/shard_map/all_gather | solution.py:371
  74.6 28.7 %all-reduce = bf16[29376]{0:T(1024)(128)(2,1)S(1)} all-reduce(bf16[29376]{0:T(1024)(128)(2,1)S(1)} %dynamic-update-slice), channel_id=2, replica_groups=mesh['section'=2,'seq'=4,'wt'=4] {'section','wt'}, use_global_device_ids=true, to_apply=%add | all-reduce | flops 29376 | bytes 117504
  111.2 37.7 %all-gather.12.cloned.1.call-done = bf16[1024,1024]{1,0:T(8,128)(2,1)} async-done(((bf16[256,1024]{1,0:T(8,128)(2,1)}), bf16[1024,1024]{1,0:T(8,128)(2,1)}) %all-gather.12.cloned.1.call-update) | async-done | bytes 2097168 | tf_op jit(solution)/shard_map/all_gather | solution.py:371
  148.9 3.8 fusion.115
  152.9 3.6 fusion.208
  169.4 4.8 collective-permute-start.3
  176.0 30.2 %all-gather.10.cloned.1.call-done = bf16[512,4384]{0,1:T(8,128)(2,1)} async-done(((bf16[128,4384]{0,1:T(8,128)(2,1)}), bf16[512,4384]{0,1:T(8,128)(2,1)}) %all-gather.10.cloned.1.call-update) | async-done | bytes 4489232 | tf_op jit(solution)/shard_map/all_gather | solution.py:371
  216.5 8.5 %collective-permute-done.4 = bf16[128,2048]{1,0:T(8,128)(2,1)S(1)} collective-permute-done((bf16[128,2048]{1,0:T(8,128)(2,1)S(1)}, bf16[128,2048]{1,0:T(8,128)(2,1)S(1)}, u32[]{:S(2)}, u32[]{:S(2)}) %collective-permute-start.4) | collective-permute-done | bytes 524320 | tf_op jit(solution)/shard_map/ppermute | solution.py:18
  226.0 4.4 collective-permute-start.5
  233.6 12.0 %shard_map.194 = f32[256,2048]{1,0:T(8,128)} custom-call(f32[256,2048]{1,0:T(8,128)} %get-tuple-element.118.refs_0_, f32[256,32]{1,0:T(8,128)} %copy.96.refs_1_.refs_2_, f32[32,256]{1,0:T(8,128)} %bitcast.167, f32[256,128]{1,0:T(8,128)} %get-tuple-element.131.refs_3_.refs_4_, f32[256,128]{1,0:T(8,128)} %get-tuple-element.130.refs_4_.refs_5_), custom_call_target="tpu_custom_call" | custom-call | flops 1073741824 | bytes 4194304 | tf_op jit(solution)/shard_map/pallas_call | solution.py:130
  245.7 6.0 multiply_reduce_fusion.15
  259.3 4.2 fusion.117
  263.6 3.6 fusion.210
  267.2 3.8 collective-permute-start.9
  273.1 3.8 fusion.20
  280.6 3.6 collective-permute-start.10
  288.1 6.5 collective-permute-done.10
  294.8 4.4 collective-permute-start.11
  301.4 7.3 collective-permute-done.11
  308.9 4.4 collective-permute-start.12
  316.5 12.1 %shard_map.195 = f32[256,2048]{1,0:T(8,128)} custom-call(f32[256,2048]{1,0:T(8,128)} %get-tuple-element.112.refs_0_, f32[256,32]{1,0:T(8,128)} %copy.99.refs_1_.refs_2_, f32[32,256]{1,0:T(8,128)} %bitcast.169, f32[256,128]{1,0:T(8,128)} %get-tuple-element.129.refs_3_.refs_4_, f32[256,128]{1,0:T(8,128)} %get-tuple-element.128.refs_4_.refs_5_), custom_call_target="tpu_custom_call" | custom-call | flops 1073741824 | bytes 4194304 | tf_op jit(solution)/shard_map/pallas_call | solution.py:130
  328.6 6.0 multiply_reduce_fusion.14
  334.7 4.1 multiply_reduce_fusion.8
  338.8 5.3 multiply_reduce_fusion.9
  345.8 11.5 %collective-permute-done.15 = bf16[128,2048]{1,0:T(8,128)(2,1)S(1)} collective-permute-done((bf16[128,2048]{1,0:T(8,128)(2,1)S(1)}, bf16[128,2048]{1,0:T(8,128)(2,1)S(1)}, u32[]{:S(2)}, u32[]{:S(2)}) %collective-permute-start.15) | collective-permute-done | bytes 524320 | tf_op jit(solution)/shard_map/ppermute | solution.py:18
  361.0 14.1 %shard_map.196 = (f32[256,2048]{1,0:T(8,128)}, f32[256,256]{1,0:T(8,128)}, f32[256,32]{1,0:T(8,128)}, f32[32,256]{1,0:T(8,128)}) custom-call(f32[256,2048]{1,0:T(8,128)} %get-tuple-element.112.refs_0_, f32[256,2048]{1,0:T(8,128)} %convert_element_type.378.refs_1_, f32[256,32]{1,0:T(8,128)} %copy.99.refs_1_.refs_2_, f32[32,256]{1,0:T(8,128)} %bitcast.170, ...), custom_call_target="tpu_custom_call" | custom-call | flops 2147483648 | bytes 6291456 | tf_op jit(solution)/shard_map/pallas_call | solution.py:149
  383.9 7.5 collective-permute-done.17
  408.4 3.5 convolution_convert_fusion
  413.3 3.7 broadcast_select_fusion.18
  431.6 15.8 %collective-permute-done.19 = bf16[128,2048]{1,0:T(8,128)(2,1)S(1)} collective-permute-done((bf16[128,2048]{1,0:T(8,128)(2,1)S(1)}, bf16[128,2048]{1,0:T(8,128)(2,1)S(1)}, u32[]{:S(2)}, u32[]{:S(2)}) %collective-permute-start.19) | collective-permute-done | bytes 524320 | tf_op jit(solution)/shard_map/ppermute | solution.py:18
  451.3 14.2 %shard_map.197 = (f32[256,2048]{1,0:T(8,128)}, f32[256,256]{1,0:T(8,128)}, f32[256,32]{1,0:T(8,128)}, f32[32,256]{1,0:T(8,128)}) custom-call(f32[256,2048]{1,0:T(8,128)} %get-tuple-element.118.refs_0_, f32[256,2048]{1,0:T(8,128)} %convert_element_type.400.refs_1_, f32[256,32]{1,0:T(8,128)} %copy.96.refs_1_.refs_2_, f32[32,256]{1,0:T(8,128)} %bitcast.168, ...), custom_call_target="tpu_custom_call" | custom-call | flops 2147483648 | bytes 6291456 | tf_op jit(solution)/shard_map/pallas_call | solution.py:149
  474.0 12.3 %collective-permute-done.21 = bf16[128,2048]{1,0:T(8,128)(2,1)S(1)} collective-permute-done((bf16[128,2048]{1,0:T(8,128)(2,1)S(1)}, bf16[128,2048]{1,0:T(8,128)(2,1)S(1)}, u32[]{:S(2)}, u32[]{:S(2)}) %collective-permute-start.21) | collective-permute-done | bytes 524320 | tf_op jit(solution)/shard_map/ppermute | solution.py:18
  487.5 4.6 multiply_add_fusion.2
  492.2 5.9 add_convert_fusion
  498.1 6.5 copy.136
  504.7 3.8 multiply_reduce_fusion.7
  519.5 7.6 collective-permute-done.24
  527.1 3.6 add_convert_fusion.1
  530.7 6.6 copy.134
  539.8 4.0 collective-permute-done.29
  548.3 4.0 collective-permute-done.28
  563.7 3.6 fusion.190
  567.4 3.7 broadcast_select_fusion.16
  574.4 44.9 %reduce-scatter.13.cloned.1.call-done = bf16[128,4384]{1,0:T(8,128)(2,1)} async-done(((bf16[512,4384]{1,0:T(8,128)(2,1)}), bf16[128,4384]{1,0:T(8,128)(2,1)}) %reduce-scatter.13.cloned.1.call-update) | async-done | bytes 1122320
  621.6 36.4 %reduce-scatter.11.cloned.1.call-done = bf16[256,1024]{1,0:T(8,128)(2,1)} async-done(((bf16[1024,1024]{1,0:T(8,128)(2,1)}), bf16[256,1024]{1,0:T(8,128)(2,1)}) %reduce-scatter.11.cloned.1.call-update) | async-done | bytes 524304 | tf_op jit(solution)/shard_map/reduce_scatter | solution.py:339
  658.0 39.1 %reduce-scatter.9.cloned.1.call-done = bf16[256,1024]{1,0:T(8,128)(2,1)} async-done(((bf16[1024,1024]{1,0:T(8,128)(2,1)}), bf16[256,1024]{1,0:T(8,128)(2,1)}) %reduce-scatter.9.cloned.1.call-update) | async-done | bytes 524304 | tf_op jit(solution)/shard_map/reduce_scatter | solution.py:339
  702.4 79.4 %psum.39 = f32[14688]{0:T(1024)S(1)} all-reduce(f32[14688]{0:T(1024)S(1)} %select_add_fusion), channel_id=1, replica_groups=mesh['section'=2,'seq'=4,'wt'=4] {'seq','wt'}, use_global_device_ids=true, to_apply=%region_40.41 | all-reduce | flops 14688 | bytes 117504 | tf_op jit(solution)/shard_map/psum | solution.py:415
  784.7 43.1 %all-reduce.4.cloned.1.call-done = (bf16[128,4384]{0,1:T(8,128)(2,1)}, bf16[128,4384]{0,1:T(8,128)(2,1)}, bf16[256,1024]{1,0:T(8,128)(2,1)}, bf16[256,1024]{1,0:T(8,128)(2,1)}) async-done(((bf16[128,4384]{0,1:T(8,128)(2,1)}, bf16[128,4384]{0,1:T(8,128)(2,1)}, bf16[256,1024]{1,0:T(8,128)(2,1)}, bf16[256,1024]{1,0:T(8,128)(2,1)}), (bf16[128,4384]{0,1:T(8,128)(2,1)}, bf16[128,4384]{0,1:T(8,128)(2,1)}, ...) | async-done | bytes 3293200 | tf_op jit(solution)/shard_map/psum | solution.py:340
  (753 shorter events, 192.6 us)
Async XLA Ops:
  7.2 65.5 %all-gather.6.cloned.1.call-start = ((), (), s32[]{:S(2)}) async-start(), calls=%async_computation.4 | async-start | bytes 5611520 | tf_op jit(solution)/shard_map/all_gather | solution.py:371
  8.7 3.0 collective-permute-start
  14.9 96.1 %all-gather.8.cloned.1.call-start = ((), (), s32[]{:S(2)}) async-start(), calls=%async_computation.5 | async-start | bytes 2621440 | tf_op jit(solution)/shard_map/all_gather | solution.py:371
  15.1 59.1 %copy-start.213 = (bf16[1,8]{1,0:T(2,128)(2,1)S(1)}, bf16[1,8]{1,0:T(2,128)(2,1)}, u32[]{:S(2)}) copy-start(bf16[1,8]{1,0:T(2,128)(2,1)} %param.17) | copy-start | bytes 52
  15.1 2.0 collective-permute-start.6
  18.3 92.1 %copy-start.41 = (bf16[2,1,256,1024]{3,2,1,0:T(8,128)(2,1)S(1)}, bf16[2,1,256,1024]{3,2,1,0:T(8,128)(2,1)}, u32[]{:S(2)}) copy-start(bf16[2,1,256,1024]{3,2,1,0:T(8,128)(2,1)} %param.11) | copy-start | bytes 3145732
  18.4 130.5 %all-gather.12.cloned.1.call-start = ((), (), s32[]{:S(2)}) async-start(), calls=%async_computation.7 | async-start | bytes 2621440 | tf_op jit(solution)/shard_map/all_gather | solution.py:371
  19.1 187.1 %all-gather.10.cloned.1.call-start = ((), (), s32[]{:S(2)}) async-start(), calls=%async_computation.6 | async-start | bytes 5611520 | tf_op jit(solution)/shard_map/all_gather | solution.py:371
  72.7 76.2 %collective-permute-start.1 = (bf16[512,4384]{0,1:T(8,128)(2,1)}, bf16[512,4384]{0,1:T(8,128)(2,1)}, u32[]{:S(2)}, u32[]{:S(2)}) collective-permute-start(bf16[512,4384]{0,1:T(8,128)(2,1)} %all-gather.6.cloned.1.call-done), channel_id=1, source_target_pairs={{0,16},{16,0},{1,17},{17,1},{2,18},{18,2},{3,19},{19,3},{4,20},{20... | collective-permute-start | bytes 13467656 | tf_op jit(solution)/shard_map/ppermute | solution.py:22
  103.4 468.6 %reduce-scatter.15.cloned.1.call-start = ((), (), s32[]{:S(2)}) async-start(), calls=%async_computation.11 | async-start | bytes 5734400
  103.6 148.1 %copy-start.155 = (f32[1,4,4,128]{3,1,2,0:T(4,128)}, f32[1,4,4,128]{3,1,2,0:T(4,128)S(1)}, u32[]{:S(2)}) copy-start(f32[1,4,4,128]{3,1,2,0:T(4,128)S(1)} %copy.139) | copy-start | bytes 24580
  105.4 153.1 %copy-start.169 = (f32[1,2,4,128]{3,1,2,0:T(2,128)}, f32[1,2,4,128]{3,1,2,0:T(2,128)S(1)}, u32[]{:S(2)}) copy-start(f32[1,2,4,128]{3,1,2,0:T(2,128)S(1)} %copy.140) | copy-start | bytes 12292
  111.1 143.6 %collective-permute-start.7 = (bf16[1024,1024]{1,0:T(8,128)(2,1)}, bf16[1024,1024]{1,0:T(8,128)(2,1)}, u32[]{:S(2)}, u32[]{:S(2)}) collective-permute-start(bf16[1024,1024]{1,0:T(8,128)(2,1)} %all-gather.8.cloned.1.call-done), channel_id=1, source_target_pairs={{0,16},{16,0},{1,17},{17,1},{2,18},{18,2},{3,19},{19,3},{4,20},{20... | collective-permute-start | bytes 6291464 | tf_op jit(solution)/shard_map/ppermute | solution.py:22
  148.9 64.4 %collective-permute-start.13 = (bf16[1024,1024]{1,0:T(8,128)(2,1)}, bf16[1024,1024]{1,0:T(8,128)(2,1)}, u32[]{:S(2)}, u32[]{:S(2)}) collective-permute-start(bf16[1024,1024]{1,0:T(8,128)(2,1)} %all-gather.12.cloned.1.call-done), channel_id=1, source_target_pairs={{0,16},{16,0},{1,17},{17,1},{2,18},{18,2},{3,19},{19,3},{4,20},{20... | collective-permute-start | bytes 6291464 | tf_op jit(solution)/shard_map/ppermute | solution.py:22
  156.5 5.2 collective-permute-start.2
  160.4 70.8 %copy-start.77 = (f32[256,32]{0,1:T(8,128)}, f32[256,32]{0,1:T(8,128)S(1)}, u32[]{:S(2)}) copy-start(f32[256,32]{0,1:T(8,128)S(1)} %fusion.75) | copy-start | bytes 98308
  169.4 39.2 %collective-permute-start.3 = (bf16[128,2048]{1,0:T(8,128)(2,1)}, bf16[128,2048]{1,0:T(8,128)(2,1)}, u32[]{:S(2)}, u32[]{:S(2)}) collective-permute-start(bf16[128,2048]{1,0:T(8,128)(2,1)} %get-tuple-element.204), channel_id=1, source_target_pairs={{0,4},{4,8},{8,12},{1,5},{5,9},{9,13},{2,6},{6,10},{10,14},{3,7},{... | collective-permute-start | bytes 1572872 | tf_op jit(solution)/shard_map/ppermute | solution.py:18
  206.2 52.7 %collective-permute-start.8 = (bf16[512,4384]{0,1:T(8,128)(2,1)}, bf16[512,4384]{0,1:T(8,128)(2,1)}, u32[]{:S(2)}, u32[]{:S(2)}) collective-permute-start(bf16[512,4384]{0,1:T(8,128)(2,1)} %all-gather.10.cloned.1.call-done), channel_id=1, source_target_pairs={{0,16},{16,0},{1,17},{17,1},{2,18},{18,2},{3,19},{19,3},{4,20},{20... | collective-permute-start | bytes 13467656 | tf_op jit(solution)/shard_map/ppermute | solution.py:22
  209.8 15.2 %collective-permute-start.4 = (bf16[128,2048]{1,0:T(8,128)(2,1)S(1)}, bf16[128,2048]{1,0:T(8,128)(2,1)S(1)}, u32[]{:S(2)}, u32[]{:S(2)}) collective-permute-start(bf16[128,2048]{1,0:T(8,128)(2,1)S(1)} %add_convert_fusion.13), channel_id=1, source_target_pairs={{0,4},{4,8},{8,12},{1,5},{5,9},{9,13},{2,6},{6,10},{10,14},{3,7},{... | collective-permute-start | bytes 1572872 | tf_op jit(solution)/shard_map/ppermute | solution.py:18
  226.0 19.7 %collective-permute-start.5 = (bf16[128,2048]{1,0:T(8,128)(2,1)}, bf16[128,2048]{1,0:T(8,128)(2,1)S(1)}, u32[]{:S(2)}, u32[]{:S(2)}) collective-permute-start(bf16[128,2048]{1,0:T(8,128)(2,1)} %add_convert_fusion.12), channel_id=1, source_target_pairs={{0,4},{4,8},{8,12},{1,5},{5,9},{9,13},{2,6},{6,10},{10,14},{3,7},{... | collective-permute-start | bytes 1572872 | tf_op jit(solution)/shard_map/ppermute | solution.py:18
  267.2 5.6 collective-permute-start.9
  280.6 14.0 %collective-permute-start.10 = (bf16[128,2048]{1,0:T(8,128)(2,1)S(1)}, bf16[128,2048]{1,0:T(8,128)(2,1)S(1)}, u32[]{:S(2)}, u32[]{:S(2)}) collective-permute-start(bf16[128,2048]{1,0:T(8,128)(2,1)S(1)} %get-tuple-element.212), channel_id=1, source_target_pairs={{0,4},{4,8},{8,12},{1,5},{5,9},{9,13},{2,6},{6,10},{10,14},{3,7},{... | collective-permute-start | bytes 1572872 | tf_op jit(solution)/shard_map/ppermute | solution.py:18
  294.8 14.0 %collective-permute-start.11 = (bf16[128,2048]{1,0:T(8,128)(2,1)S(1)}, bf16[128,2048]{1,0:T(8,128)(2,1)S(1)}, u32[]{:S(2)}, u32[]{:S(2)}) collective-permute-start(bf16[128,2048]{1,0:T(8,128)(2,1)S(1)} %add_convert_fusion.11), channel_id=1, source_target_pairs={{0,4},{4,8},{8,12},{1,5},{5,9},{9,13},{2,6},{6,10},{10,14},{3,7},{... | collective-permute-start | bytes 1572872 | tf_op jit(solution)/shard_map/ppermute | solution.py:18
  308.9 19.7 %collective-permute-start.12 = (bf16[128,2048]{1,0:T(8,128)(2,1)S(1)}, bf16[128,2048]{1,0:T(8,128)(2,1)S(1)}, u32[]{:S(2)}, u32[]{:S(2)}) collective-permute-start(bf16[128,2048]{1,0:T(8,128)(2,1)S(1)} %add_convert_fusion.10), channel_id=1, source_target_pairs={{0,4},{4,8},{8,12},{1,5},{5,9},{9,13},{2,6},{6,10},{10,14},{3,7},{... | collective-permute-start | bytes 1572872 | tf_op jit(solution)/shard_map/ppermute | solution.py:18
  344.5 12.8 %collective-permute-start.15 = (bf16[128,2048]{1,0:T(8,128)(2,1)S(1)}, bf16[128,2048]{1,0:T(8,128)(2,1)S(1)}, u32[]{:S(2)}, u32[]{:S(2)}) collective-permute-start(bf16[128,2048]{1,0:T(8,128)(2,1)S(1)} %get-tuple-element.215), channel_id=1, source_target_pairs={{4,0},{8,4},{12,8},{5,1},{9,5},{13,9},{6,2},{10,6},{14,10},{7,3},{... | collective-permute-start | bytes 1572872 | tf_op jit(solution)/shard_map/ppermute | solution.py:18
  358.2 19.3 %collective-permute-start.16 = (bf16[128,2048]{1,0:T(8,128)(2,1)}, bf16[128,2048]{1,0:T(8,128)(2,1)}, u32[]{:S(2)}, u32[]{:S(2)}) collective-permute-start(bf16[128,2048]{1,0:T(8,128)(2,1)} %add_convert_fusion.9), channel_id=1, source_target_pairs={{4,0},{8,4},{12,8},{5,1},{9,5},{13,9},{6,2},{10,6},{14,10},{7,3},{... | collective-permute-start | bytes 1572872 | tf_op jit(solution)/shard_map/ppermute | solution.py:18
  379.0 12.5 %collective-permute-start.17 = (bf16[128,2048]{1,0:T(8,128)(2,1)S(1)}, bf16[128,2048]{1,0:T(8,128)(2,1)S(1)}, u32[]{:S(2)}, u32[]{:S(2)}) collective-permute-start(bf16[128,2048]{1,0:T(8,128)(2,1)S(1)} %add_convert_fusion.8), channel_id=1, source_target_pairs={{4,0},{8,4},{12,8},{5,1},{9,5},{13,9},{6,2},{10,6},{14,10},{7,3},{... | collective-permute-start | bytes 1572872 | tf_op jit(solution)/shard_map/ppermute | solution.py:18
  399.1 7.0 collective-permute-start.18
  426.4 65.7 %collective-permute-start.25 = (bf16[512,4384]{0,1:T(8,128)(2,1)}, bf16[512,4384]{0,1:T(8,128)(2,1)}, u32[]{:S(2)}, u32[]{:S(2)}) collective-permute-start(bf16[512,4384]{0,1:T(8,128)(2,1)} %convolution_convert_fusion), channel_id=1, source_target_pairs={{0,16},{16,0},{1,17},{17,1},{2,18},{18,2},{3,19},{19,3},{4,20},{20... | collective-permute-start | bytes 13467656 | tf_op jit(solution)/shard_map/ppermute | solution.py:22
  430.3 17.1 %collective-permute-start.19 = (bf16[128,2048]{1,0:T(8,128)(2,1)S(1)}, bf16[128,2048]{1,0:T(8,128)(2,1)S(1)}, u32[]{:S(2)}, u32[]{:S(2)}) collective-permute-start(bf16[128,2048]{1,0:T(8,128)(2,1)S(1)} %get-tuple-element.222), channel_id=1, source_target_pairs={{4,0},{8,4},{12,8},{5,1},{9,5},{13,9},{6,2},{10,6},{14,10},{7,3},{... | collective-permute-start | bytes 1572872 | tf_op jit(solution)/shard_map/ppermute | solution.py:18
  448.3 20.0 %collective-permute-start.20 = (bf16[128,2048]{1,0:T(8,128)(2,1)}, bf16[128,2048]{1,0:T(8,128)(2,1)}, u32[]{:S(2)}, u32[]{:S(2)}) collective-permute-start(bf16[128,2048]{1,0:T(8,128)(2,1)} %add_convert_fusion.7), channel_id=1, source_target_pairs={{4,0},{8,4},{12,8},{5,1},{9,5},{13,9},{6,2},{10,6},{14,10},{7,3},{... | collective-permute-start | bytes 1572872 | tf_op jit(solution)/shard_map/ppermute | solution.py:18
  469.9 16.4 %collective-permute-start.21 = (bf16[128,2048]{1,0:T(8,128)(2,1)S(1)}, bf16[128,2048]{1,0:T(8,128)(2,1)S(1)}, u32[]{:S(2)}, u32[]{:S(2)}) collective-permute-start(bf16[128,2048]{1,0:T(8,128)(2,1)S(1)} %add_convert_fusion.6), channel_id=1, source_target_pairs={{4,0},{8,4},{12,8},{5,1},{9,5},{13,9},{6,2},{10,6},{14,10},{7,3},{... | collective-permute-start | bytes 1572872 | tf_op jit(solution)/shard_map/ppermute | solution.py:18
  504.6 114.6 %reduce-scatter.13.cloned.1.call-start = ((), (), s32[]{:S(2)}) async-start(), calls=%async_computation.10 | async-start | bytes 5734400
  508.6 8.0 collective-permute-start.22
  519.5 7.6 collective-permute-start.24
  537.3 120.7 %reduce-scatter.11.cloned.1.call-start = ((), (), s32[]{:S(2)}) async-start(), calls=%async_computation.9 | async-start | bytes 2621440 | tf_op jit(solution)/shard_map/reduce_scatter | solution.py:339
  539.6 4.2 collective-permute-start.29
  546.0 151.1 %reduce-scatter.9.cloned.1.call-start = ((), (), s32[]{:S(2)}) async-start(), calls=%async_computation.8 | async-start | bytes 2621440 | tf_op jit(solution)/shard_map/reduce_scatter | solution.py:339
  548.0 4.2 collective-permute-start.28
  554.4 273.4 %all-reduce.4.cloned.1.call-start = ((), (), s32[]{:S(2)}) async-start(), calls=%async_computation.12 | async-start | bytes 6586368 | tf_op jit(solution)/shard_map/psum | solution.py:340
  559.2 2.1 collective-permute-start.14
  621.6 76.5 %copy-start.119 = (f32[256,512]{1,0:T(8,128)S(1)}, f32[256,512]{1,0:T(8,128)}, u32[]{:S(2)}) copy-start(f32[256,512]{1,0:T(8,128)} %copy-done.118) | copy-start | bytes 1572868
  700.6 1.8 collective-permute-start.32
  701.9 135.9 %collective-permute-start.23 = (bf16[256,1024]{1,0:T(8,128)(2,1)}, bf16[256,1024]{1,0:T(8,128)(2,1)S(1)}, u32[]{:S(2)}, u32[]{:S(2)}) collective-permute-start(bf16[256,1024]{1,0:T(8,128)(2,1)} %get-tuple-element.107), channel_id=1, source_target_pairs={{0,16},{16,0},{1,17},{17,1},{2,18},{18,2},{3,19},{19,3},{4,20},{20... | collective-permute-start | bytes 1572872 | tf_op jit(solution)/shard_map/ppermute | solution.py:22
  827.8 14.9 %collective-permute-start.26 = (bf16[128,4384]{0,1:T(8,128)(2,1)}, bf16[128,4384]{0,1:T(8,128)(2,1)S(1)}, u32[]{:S(2)}, u32[]{:S(2)}) collective-permute-start(bf16[128,4384]{0,1:T(8,128)(2,1)} %get-tuple-element.97), channel_id=1, source_target_pairs={{16,0},{17,1},{18,2},{19,3},{20,4},{21,5},{22,6},{23,7},{24,8},{25... | collective-permute-start | bytes 3366920 | tf_op jit(solution)/shard_map/ppermute | solution.py:344
  829.1 13.6 %collective-permute-start.27 = (bf16[128,4384]{0,1:T(8,128)(2,1)}, bf16[128,4384]{0,1:T(8,128)(2,1)S(1)}, u32[]{:S(2)}, u32[]{:S(2)}) collective-permute-start(bf16[128,4384]{0,1:T(8,128)(2,1)} %get-tuple-element.98), channel_id=1, source_target_pairs={{0,16},{1,17},{2,18},{3,19},{4,20},{5,21},{6,22},{7,23},{8,24},{9,... | collective-permute-start | bytes 3366920 | tf_op jit(solution)/shard_map/ppermute | solution.py:345
  832.9 8.1 collective-permute-start.30
  834.2 6.8 collective-permute-start.31
  (221 other events, 2079.9 us)
Sparse Core Ops, SparseCore 0:
  15.0 57.6 all-gather.5
  75.1 35.7 all-gather.7
  113.4 35.4 all-gather.11
  151.1 55.0 all-gather.9
  504.8 55.5 reduce-scatter.14
  563.3 55.9 reduce-scatter.12
  622.8 35.1 reduce-scatter.10
  661.8 35.2 reduce-scatter.8
  699.7 128.0 all-reduce.3

commit v2 on v1

--- a/solution.py
+++ b/solution.py
@@ -20,6 +20,51 @@
 
 def swapped(block):
     return lax.ppermute(block, "section", [(0, 1), (1, 0)])
+
+
+def crossed(block, axis, bit):
+    devices = range(lax.axis_size(axis))
+    return lax.ppermute(block, axis, [(i, i ^ bit) for i in devices])
+
+
+def bits_of(axis):
+    count = lax.axis_size(axis)
+    return [1 << k for k in range(count.bit_length() - 1)]
+
+
+def has_bit(axis, bit):
+    return (lax.axis_index(axis) // bit) % 2 == 1
+
+
+def gather_rows(block, axis, order):
+    rows, columns = block.shape
+    done = []
+    for bit in order:
+        recv, high = crossed(block, axis, bit), has_bit(axis, bit)
+        at = sum(1 for other in done if other > bit)
+        block = jnp.stack([jnp.where(high, recv, block), jnp.where(high, block, recv)], axis=at)
+        done.append(bit)
+    return block.reshape(-1, columns)
+
+
+def scatter_rows(total, axis, order):
+    rows, columns = total.shape
+    left = sorted(order, reverse=True)
+    total = total.reshape((2,) * len(left) + (rows >> len(left), columns))
+    for bit in order:
+        at = left.index(bit)
+        left.remove(bit)
+        low = lax.index_in_dim(total, 0, at, keepdims=False)
+        top = lax.index_in_dim(total, 1, at, keepdims=False)
+        high = has_bit(axis, bit)
+        recv = crossed(jnp.where(high, low, top), axis, bit)
+        total = (jnp.where(high, top, low).astype(F32) + recv.astype(F32)).astype(BF16)
+    return total
+
+
+def sum_rows(total, axis):
+    order = bits_of(axis)
+    return gather_rows(scatter_rows(total, axis, order), axis, order[::-1])
 
 
 def rms_scale(values, gain):
@@ -208,10 +253,12 @@
     length = hidden.shape[0]
     normed = rms_scale(hidden, gain_in).astype(BF16)
     normed_mine, normed_other = split_halves(normed, parts, first)
-    project = dot(normed_mine, win_mine, ROWS_COLS) + dot(normed_other, win_other, ROWS_COLS)
-    gate = project[:, :inner]
-    v = project[:, inner : inner + conv].astype(BF16)
-    dt_raw = project[:, inner + conv :].astype(BF16).astype(F32)
+    gate, project = (
+        dot(normed_mine, mine, ROWS_COLS) + dot(normed_other, other, ROWS_COLS)
+        for mine, other in zip(win_mine, win_other)
+    )
+    v = project[:, :conv].astype(BF16)
+    dt_raw = project[:, conv:].astype(BF16).astype(F32)
     halo = shifted(v[length - taps + 1 :], "seq", 1)
     padded = jnp.concatenate([halo, v], axis=0).astype(F32)
     pre = conv_bias
@@ -278,6 +325,7 @@
     )
     _, post_pull = jax.vjp(post_norm, mixed.astype(F32), gate, gain_out)
     grad_mixed, grad_gate, grad_gain_out = post_pull(grad_scaled)
+    grad_gate = grad_gate.astype(BF16)
     dy = grad_mixed.astype(BF16).astype(F32)
     dy_cum = dy * cum_w
     a_term = dot(c, dy_cum, ROWS_ROWS)
@@ -311,18 +359,16 @@
         [jnp.sum(grad_pre * padded[k : k + length], axis=0) for k in range(taps)]
     )
     grad_conv_bias = jnp.sum(grad_pre, axis=0)
-    grad_project = jnp.concatenate(
-        [grad_gate.astype(BF16), grad_v.astype(BF16), grad_dt_raw.astype(BF16)], axis=1
-    )
+    grad_rest = jnp.concatenate([grad_v.astype(BF16), grad_dt_raw.astype(BF16)], axis=1)
     grad_normed = join_halves(
-        dot(grad_project, win_mine, COLS_COLS),
-        dot(grad_project, win_other, COLS_COLS),
+        dot(grad_gate, win_mine[0], COLS_COLS) + dot(grad_rest, win_mine[1], COLS_COLS),
+        dot(grad_gate, win_other[0], COLS_COLS) + dot(grad_rest, win_other[1], COLS_COLS),
         parts,
         first,
     )
-    grad_win = (
-        dot(normed_mine, grad_project, ROWS_ROWS),
-        dot(normed_other, grad_project, ROWS_ROWS).astype(BF16),
+    grad_win = tuple(
+        (dot(normed_mine, part, ROWS_ROWS), dot(normed_other, part, ROWS_ROWS).astype(BF16))
+        for part in (grad_gate, grad_rest)
     )
     _, norm_pull = jax.vjp(rms_scale, hidden, gain_in)
     grad_hidden, grad_gain_in = norm_pull(grad_normed)
@@ -333,11 +379,38 @@
     return (upstream_b.astype(F32) + grad_hidden).astype(BF16), grad_win, grad_wout, grad_small
 
 
-def reduced(grad):
+def both_cores(grad):
     mine, other = grad
-    both = (mine + swapped(other).astype(F32)).astype(BF16)
-    share = lax.psum_scatter(both, "wt", scatter_dimension=0, tiled=True)
-    return lax.psum(share, "seq")
+    return (mine + swapped(other).astype(F32)).astype(BF16)
+
+
+def reduced_ahead(both):
+    return lax.psum(lax.psum_scatter(both, "wt", scatter_dimension=0, tiled=True), "seq")
+
+
+def reduced_last(gate, rest, out):
+    order = bits_of("wt")
+    wide = LANES * (rest.shape[1] // (2 * LANES))
+    gate = scatter_rows(gate, "wt", order)
+    out = scatter_rows(out, "wt", order[::-1])
+    rows = gate.shape[0]
+    pieces = [gate] + [out[k : k + rows] for k in range(0, out.shape[0], rows)]
+    early = sum_rows(jnp.concatenate(pieces, axis=1), "seq")
+    late = jnp.concatenate(
+        [
+            scatter_rows(rest[:, :wide], "wt", order),
+            scatter_rows(rest[:, wide:], "wt", order[::-1]),
+        ],
+        axis=1,
+    )
+    late = sum_rows(late, "seq")
+    inner = gate.shape[1]
+    columns = out.shape[1]
+    total_in = jnp.concatenate([early[:, :inner], late], axis=1)
+    total_out = jnp.concatenate(
+        [early[:, at : at + columns] for at in range(inner, early.shape[1], columns)], axis=0
+    )
+    return total_in, total_out
 
 
 def own_layer(layers, first):
@@ -367,13 +440,19 @@
         recv = swapped(lax.dynamic_slice_in_dim(weight[0], (1 - section) * rows, rows, 0))
         return jnp.where(first, keep, recv), jnp.where(first, recv, keep)
 
+    inner = out_weight.shape[1] * parts
+    order = bits_of("wt")
+
     def gathered(half):
         mine = lax.all_gather(half, "wt", axis=0, tiled=True)
         return mine, swapped(mine)
 
+    def columns(pair):
+        return tuple((whole[:, :inner], whole[:, inner:]) for whole in pair)
+
     win_halves, wout_halves = halves(in_weight), halves(out_weight)
     flat = jnp.concatenate([shard[0].reshape(-1) for shard in small_shards])
-    packed = lax.all_gather(flat, ("section", "wt"), axis=0, tiled=False)
+    packed = gather_rows(gather_rows(flat[None], "wt", order), "section", [1])
     packed = packed.reshape(2, parts, -1).astype(F32)
     smalls = []
     for layer in range(2):
@@ -388,11 +467,17 @@
             else:
                 small.append(piece.reshape(-1))
         smalls.append(tuple(small))
-    win0 = gathered(win_halves[0])
+    win0_mine = (
+        gather_rows(win_halves[0][:, :inner], "wt", order[::-1]),
+        gather_rows(win_halves[0][:, inner:], "wt", order),
+    )
+    win0 = (win0_mine, tuple(swapped(part) for part in win0_mine))
     wout0 = gathered(wout_halves[0])
-    win1 = gathered(win_halves[1])
-    wout1 = gathered(wout_halves[1])
-    weights = ((win0, wout0), (win1, wout1))
+    next_half, _ = lax.optimization_barrier((win_halves[1], wout0[0]))
+    win1 = gathered(next_half)
+    next_half, _ = lax.optimization_barrier((wout_halves[1], win1[0]))
+    wout1 = gathered(next_half)
+    weights = ((win0, wout0), (columns(win1), wout1))
 
     own_tokens = lax.dynamic_index_in_dim(tokens, section, 0, keepdims=False)[0]
     own_cotangent = lax.dynamic_index_in_dim(cotangent, section, 0, keepdims=False)[0]
@@ -402,17 +487,24 @@
     back1, gwin1, gwout1, gsmall1 = layer_backward(
         own_cotangent, saved1, weights[1], smalls[1], first, parts
     )
-    sum_wout1, sum_win1 = reduced(gwout1), reduced(gwin1)
+    both_wout1 = both_cores(gwout1)
+    both_win1 = jnp.concatenate([both_cores(part) for part in gwin1], axis=1)
+    back1, both_wout1, both_win1 = lax.optimization_barrier((back1, both_wout1, both_win1))
+    sum_wout1, sum_win1 = reduced_ahead(both_wout1), reduced_ahead(both_win1)
     back0, gwin0, gwout0, gsmall0 = layer_backward(
         back1, saved0, weights[0], smalls[0], first, parts
     )
-    sum_wout0, sum_win0 = reduced(gwout0), reduced(gwin0)
+    sum_win0, sum_wout0 = reduced_last(
+        both_cores(gwin0[0]), both_cores(gwin0[1]), both_cores(gwout0)
+    )
     input_grads = by_layer((back0, back1), first)
 
     flat0 = jnp.concatenate([g.reshape(-1) for g in gsmall0])
     flat1 = jnp.concatenate([g.reshape(-1) for g in gsmall1])
     total = jnp.where(first, flat0, flat1) + swapped(jnp.where(first, flat1, flat0))
-    total = lax.psum(total, ("seq", "wt"))
+    for axis in ("wt", "seq"):
+        for bit in bits_of(axis):
+            total = total + crossed(total, axis, bit)
     small_out, at = [], 0
     for g in gsmall0:
         piece = total[at : at + g.size].reshape(g.shape)

time: 864 us -> 851 us (0.985)
  blocking collectives: 108 us -> 0 us
  local copies, waits for them, and re-layouts: 61.6 us -> 135 us
  waiting for transfers between devices: 376 us -> 324 us
  starting transfers between devices: 54.9 us -> 89.8 us
  other arithmetic: 61.3 us -> 92.9 us
    ppermute x0 -> x27, waiting for transfers between devices: none -> 157 us  [crossed(): return lax.ppermute(block, axis, [(i, i ^ bit) for i in devices])]
    all_gather x4 -> x3, waiting for transfers between devices: 121 us -> 21.5 us  [gathered(): mine = lax.all_gather(half, 'wt', axis=0, tiled=True)]
    psum x1 -> x0, blocking collectives: 79.4 us -> none  [local(): total = lax.psum(total, ('seq', 'wt'))]
    reduce_scatter x2, waiting for transfers between devices: 75.4 us -> 0.04 us  [reduced_ahead(): lax.psum_scatter(both, 'wt', scatter_dimension=0, tiled=True)]
    unnamed x11 -> x6, waiting for transfers between devices: 45.7 us -> 0.1 us
    ppermute x0 -> x27, starting transfers between devices: none -> 36.2 us  [crossed(): return lax.ppermute(block, axis, [(i, i ^ bit) for i in devices])]
    unnamed x1 -> x0, blocking collectives: 28.7 us -> none
    ppermute x13 -> x16, waiting for transfers between devices: 21 us -> 0.04 us  [swapped(): return lax.ppermute(block, 'section', [(0, 1), (1, 0)])]
  transfers between devices with their start and end apart: 42 -> 69, of which waited for: 20 -> 30; matrix products, arithmetic and copies ran while one was open for 18% -> 37% of each run, Pallas kernels for 6% -> 6%
where the time goes in v2:
time: 851 us; the launch traced here: 839 us
  waiting for transfers between devices  324 us (38%)
  local copies, waits for them, and re-layouts  135 us (16%)
  matrix products  127 us (15%)
  other arithmetic  92.9 us (11%)
  starting transfers between devices  89.8 us (11%)
  Pallas kernels  52.8 us (6%)
  between operations  17.9 us (2%)
    ppermute x27, waiting for transfers between devices, crossed(): return lax.ppermute(block, axis, [(i, i ^ bit) for i in devices])  157 us
    dot_general x58, matrix products, dot(): lax.dot_general(a.astype(BF16), b.astype(BF16), (over, ((), ())), preferr...  108 us
    ppermute x16, waiting for transfers between devices, shifted(): return lax.ppermute(block, axis, route)  84.6 us
    psum x1, waiting for transfers between devices, reduced_ahead(): lax.psum(lax.psum_scatter(both, 'wt', scatter_dimension=0, tiled=True), '...  60.5 us
    ppermute x16, starting transfers between devices, shifted(): return lax.ppermute(block, axis, route)  40.4 us
    ppermute x27, starting transfers between devices, crossed(): return lax.ppermute(block, axis, [(i, i ^ bit) for i in devices])  36.2 us
    unnamed x424, local copies, waits for them, and re-layouts  33.2 us
    pallas_call x2, Pallas kernels, within_back(): pl.pallas_call(lambda *refs: within_back_kernel(head_size, *refs), grid=(...  28.7 us
  transfers between devices with their start and end apart: 69, of which 30 were waited for; matrix products, arithmetic and copies ran while one was open for 37% of the time, Pallas kernels for 6%

profile of v2, /device:TPU:0, one launch (start us, length us, event | category | flops | bytes accessed | tf_op | source)
XLA Modules:
  0.0 838.7 jit_solution(10642249388722757376)
XLA Ops:
  29.7 13.1 %collective-permute-done.4 = bf16[128,2336]{0,1:T(8,128)(2,1)S(1)} collective-permute-done((bf16[128,2336]{0,1:T(8,128)(2,1)S(1)}, bf16[128,2336]{0,1:T(8,128)(2,1)S(1)}, u32[]{:S(2)}, u32[]{:S(2)}) %collective-permute-start.4) | collective-permute-done | bytes 598048 | tf_op jit(solution)/shard_map/ppermute | solution.py:27
  53.5 29.3 %collective-permute-done.5 = bf16[2,128,2336]{1,2,0:T(8,128)(2,1)} collective-permute-done((bf16[2,128,2336]{1,2,0:T(8,128)(2,1)}, bf16[2,128,2336]{1,2,0:T(8,128)(2,1)}, u32[]{:S(2)}, u32[]{:S(2)}) %collective-permute-start.5) | collective-permute-done | bytes 1196064 | tf_op jit(solution)/shard_map/ppermute | solution.py:27
  90.0 13.2 %collective-permute-done.11 = bf16[128,2048]{1,0:T(8,128)(2,1)} collective-permute-done((bf16[128,2048]{1,0:T(8,128)(2,1)S(1)}, bf16[128,2048]{1,0:T(8,128)(2,1)}, u32[]{:S(2)}, u32[]{:S(2)}) %collective-permute-start.11) | collective-permute-done | bytes 524320 | tf_op jit(solution)/shard_map/ppermute | solution.py:27
  133.0 3.6 collective-permute-start.7
  142.2 3.4 multiply_convert_fusion.13
  146.6 3.6 collective-permute-start.8
  158.2 5.2 collective-permute-start.9
  190.7 3.6 fusion.253
  196.8 12.0 %shard_map.194 = f32[256,2048]{1,0:T(8,128)} custom-call(f32[256,2048]{1,0:T(8,128)} %get-tuple-element.137.refs_0_, f32[256,32]{1,0:T(8,128)} %copy.231.refs_1_.refs_2_, f32[32,256]{1,0:T(8,128)} %bitcast.370, f32[256,128]{1,0:T(8,128)} %get-tuple-element.152.refs_3_.refs_4_, f32[256,128]{1,0:T(8,128)} %get-tuple-element.151.refs_4_.refs_5_), custom_call_target="tpu_custom_call" | custom-call | flops 1073741824 | bytes 4194304 | tf_op jit(solution)/shard_map/pallas_call | solution.py:175
  208.8 6.5 copy.234
  218.6 5.7 multiply_reduce_fusion.15
  238.1 21.5 %all-gather.8.cloned.1.call-done = bf16[1024,1024]{1,0:T(8,128)(2,1)} async-done(((bf16[256,1024]{1,0:T(8,128)(2,1)}), bf16[1024,1024]{1,0:T(8,128)(2,1)}) %all-gather.8.cloned.1.call-update) | async-done | bytes 2097168 | tf_op jit(solution)/shard_map/all_gather | solution.py:447
  259.6 3.6 fusion.99
  265.9 3.4 collective-permute-start.17
  278.6 3.4 multiply_convert_fusion.11
  283.1 4.2 collective-permute-start.18
  289.7 12.1 %shard_map.195 = f32[256,2048]{1,0:T(8,128)} custom-call(f32[256,2048]{1,0:T(8,128)} %get-tuple-element.131.refs_0_, f32[256,32]{1,0:T(8,128)} %copy.237.refs_1_.refs_2_, f32[32,256]{1,0:T(8,128)} %bitcast.372, f32[256,128]{1,0:T(8,128)} %get-tuple-element.150.refs_3_.refs_4_, f32[256,128]{1,0:T(8,128)} %get-tuple-element.149.refs_4_.refs_5_), custom_call_target="tpu_custom_call" | custom-call | flops 1073741824 | bytes 4194304 | tf_op jit(solution)/shard_map/pallas_call | solution.py:175
  308.5 8.5 %collective-permute-done.19 = bf16[128,2048]{1,0:T(8,128)(2,1)S(1)} collective-permute-done((bf16[128,2048]{1,0:T(8,128)(2,1)S(1)}, bf16[128,2048]{1,0:T(8,128)(2,1)S(1)}, u32[]{:S(2)}, u32[]{:S(2)}) %collective-permute-start.19) | collective-permute-done | bytes 524320 | tf_op jit(solution)/shard_map/ppermute | solution.py:18
  317.2 4.4 collective-permute-start.20
  321.7 10.2 %collective-permute-done.20 = bf16[128,2048]{1,0:T(8,128)(2,1)S(1)} collective-permute-done((bf16[128,2048]{1,0:T(8,128)(2,1)S(1)}, bf16[128,2048]{1,0:T(8,128)(2,1)S(1)}, u32[]{:S(2)}, u32[]{:S(2)}) %collective-permute-start.20) | collective-permute-done | bytes 524320 | tf_op jit(solution)/shard_map/ppermute | solution.py:18
  333.2 3.6 multiply_reduce_fusion.14
  346.7 3.3 broadcast_select_fusion.12
  350.1 14.2 %shard_map.196 = (f32[256,2048]{1,0:T(8,128)}, f32[256,256]{1,0:T(8,128)}, f32[256,32]{1,0:T(8,128)}, f32[32,256]{1,0:T(8,128)}) custom-call(f32[256,2048]{1,0:T(8,128)} %get-tuple-element.131.refs_0_, f32[256,2048]{1,0:T(8,128)} %convert_element_type.539.refs_1_, f32[256,32]{1,0:T(8,128)} %copy.237.refs_1_.refs_2_, f32[32,256]{1,0:T(8,128)} %bitcast.373, ...), custom_call_target="tpu_custom_call" | custom-call | flops 2147483648 | bytes 6291456 | tf_op jit(solution)/shard_map/pallas_call | solution.py:194
  367.1 3.6 convolution_convert_fusion.5
  373.2 8.3 collective-permute-done.23
  386.7 11.6 %collective-permute-done.24 = bf16[128,2048]{1,0:T(8,128)(2,1)S(1)} collective-permute-done((bf16[128,2048]{1,0:T(8,128)(2,1)S(1)}, bf16[128,2048]{1,0:T(8,128)(2,1)S(1)}, u32[]{:S(2)}, u32[]{:S(2)}) %collective-permute-start.24) | collective-permute-done | bytes 524320 | tf_op jit(solution)/shard_map/ppermute | solution.py:18
  400.5 12.7 %collective-permute-done.25 = bf16[128,2048]{1,0:T(8,128)(2,1)S(1)} collective-permute-done((bf16[128,2048]{1,0:T(8,128)(2,1)S(1)}, bf16[128,2048]{1,0:T(8,128)(2,1)S(1)}, u32[]{:S(2)}, u32[]{:S(2)}) %collective-permute-start.25) | collective-permute-done | bytes 524320 | tf_op jit(solution)/shard_map/ppermute | solution.py:18
  441.3 4.0 copy.246
  445.2 4.3 add_convert_fusion.5
  463.2 3.4 multiply_reduce_fusion.11
  475.2 14.5 %shard_map.197 = (f32[256,2048]{1,0:T(8,128)}, f32[256,256]{1,0:T(8,128)}, f32[256,32]{1,0:T(8,128)}, f32[32,256]{1,0:T(8,128)}) custom-call(f32[256,2048]{1,0:T(8,128)} %get-tuple-element.137.refs_0_, f32[256,2048]{1,0:T(8,128)} %convert_element_type.570.refs_1_, f32[256,32]{1,0:T(8,128)} %copy.231.refs_1_.refs_2_, f32[32,256]{1,0:T(8,128)} %bitcast.371, ...), custom_call_target="tpu_custom_call" | custom-call | flops 2147483648 | bytes 6291456 | tf_op jit(solution)/shard_map/pallas_call | solution.py:194
  491.4 3.6 convolution_convert_fusion.4
  501.4 12.6 %collective-permute-done.31 = bf16[128,2048]{1,0:T(8,128)(2,1)S(1)} collective-permute-done((bf16[128,2048]{1,0:T(8,128)(2,1)S(1)}, bf16[128,2048]{1,0:T(8,128)(2,1)S(1)}, u32[]{:S(2)}, u32[]{:S(2)}) %collective-permute-start.31) | collective-permute-done | bytes 524320 | tf_op jit(solution)/shard_map/ppermute | solution.py:18
  516.2 13.9 %collective-permute-done.32 = bf16[128,2048]{1,0:T(8,128)(2,1)S(1)} collective-permute-done((bf16[128,2048]{1,0:T(8,128)(2,1)S(1)}, bf16[128,2048]{1,0:T(8,128)(2,1)S(1)}, u32[]{:S(2)}, u32[]{:S(2)}) %collective-permute-start.32) | collective-permute-done | bytes 524320 | tf_op jit(solution)/shard_map/ppermute | solution.py:18
  542.5 3.7 collective-permute-done.33
  546.2 5.2 fusion.7
  566.1 6.6 copy.296
  597.9 30.1 %collective-permute-done.39 = bf16[2,256,1024]{2,1,0:T(8,128)(2,1)} collective-permute-done((bf16[2,256,1024]{2,1,0:T(8,128)(2,1)}, bf16[2,256,1024]{2,1,0:T(8,128)(2,1)}, u32[]{:S(2)}, u32[]{:S(2)}) %collective-permute-start.39) | collective-permute-done | bytes 1048608 | tf_op jit(solution)/shard_map/ppermute | solution.py:27
  635.3 18.6 %collective-permute-done.40 = bf16[256,1024]{1,0:T(8,128)(2,1)S(1)} collective-permute-done((bf16[256,1024]{1,0:T(8,128)(2,1)S(1)}, bf16[256,1024]{1,0:T(8,128)(2,1)S(1)}, u32[]{:S(2)}, u32[]{:S(2)}) %collective-permute-start.40) | collective-permute-done | bytes 524320 | tf_op jit(solution)/shard_map/ppermute | solution.py:27
  675.6 10.0 %collective-permute-done.42 = bf16[32,4096]{1,0:T(8,128)(2,1)S(1)} collective-permute-done((bf16[32,4096]{1,0:T(8,128)(2,1)S(1)}, bf16[32,4096]{1,0:T(8,128)(2,1)S(1)}, u32[]{:S(2)}, u32[]{:S(2)}) %collective-permute-start.42) | collective-permute-done | bytes 262176 | tf_op jit(solution)/shard_map/ppermute | solution.py:27
  691.2 4.3 collective-permute-done.47
  701.6 5.0 collective-permute-done.50
  709.5 3.6 collective-permute-done.51
  714.9 10.0 %collective-permute-done.44 = bf16[2,32,4096]{2,1,0:T(8,128)(2,1)S(1)} collective-permute-done((bf16[2,32,4096]{2,1,0:T(8,128)(2,1)S(1)}, bf16[2,32,4096]{2,1,0:T(8,128)(2,1)S(1)}, u32[]{:S(2)}, u32[]{:S(2)}) %collective-permute-start.44) | collective-permute-done | bytes 524320 | tf_op jit(solution)/shard_map/ppermute | solution.py:27
  728.5 3.6 collective-permute-done.53
  739.6 60.5 %all-reduce.3.cloned.1.call-done = (bf16[128,4384]{1,0:T(8,128)(2,1)}, bf16[256,1024]{1,0:T(8,128)(2,1)}) async-done(((bf16[128,4384]{1,0:T(8,128)(2,1)}, bf16[256,1024]{1,0:T(8,128)(2,1)}), (bf16[128,4384]{1,0:T(8,128)(2,1)}, bf16[256,1024]{1,0:T(8,128)(2,1)})) %all-reduce.3.cloned.1.call-update) | async-done | bytes 1646608 | tf_op jit(solution)/shard_map/psum | solution.py:388
  806.1 4.7 collective-permute-start.57
  825.8 5.9 copy.279
  (828 shorter events, 365.1 us)
Async XLA Ops:
  7.2 117.9 %all-gather.4.cloned.1.call-start = ((), (), s32[]{:S(2)}) async-start(), calls=%async_computation.2 | async-start | bytes 2621440 | tf_op jit(solution)/shard_map/all_gather | solution.py:447
  9.1 39.9 %collective-permute-start.14 = (bf16[256,1024]{1,0:T(8,128)(2,1)}, bf16[256,1024]{1,0:T(8,128)(2,1)}, u32[]{:S(2)}, u32[]{:S(2)}) collective-permute-start(bf16[256,1024]{1,0:T(8,128)(2,1)} %dynamic-slice_bitcast_fusion.1), channel_id=1, source_target_pairs={{0,16},{16,0},{1,17},{17,1},{2,18},{18,2},{3,19},{19,3},{4,20},{20... | collective-permute-start | bytes 1572872 | tf_op jit(solution)/shard_map/ppermute | solution.py:22
  26.9 16.0 %collective-permute-start.4 = (bf16[128,2336]{0,1:T(8,128)(2,1)S(1)}, bf16[128,2336]{0,1:T(8,128)(2,1)S(1)}, u32[]{:S(2)}, u32[]{:S(2)}) collective-permute-start(bf16[128,2336]{0,1:T(8,128)(2,1)S(1)} %copy.222), channel_id=1, source_target_pairs={{0,1},{1,0},{2,3},{3,2},{4,5},{5,4},{6,7},{7,6},{8,9},{9,8},{10,11... | collective-permute-start | bytes 1794056 | tf_op jit(solution)/shard_map/ppermute | solution.py:27
  46.8 36.0 %collective-permute-start.5 = (bf16[2,128,2336]{1,2,0:T(8,128)(2,1)}, bf16[2,128,2336]{1,2,0:T(8,128)(2,1)}, u32[]{:S(2)}, u32[]{:S(2)}) collective-permute-start(bf16[2,128,2336]{1,2,0:T(8,128)(2,1)} %copy.225), channel_id=1, source_target_pairs={{0,2},{1,3},{2,0},{3,1},{4,6},{5,7},{6,4},{7,5},{8,10},{9,11},{10,... | collective-permute-start | bytes 3588104 | tf_op jit(solution)/shard_map/ppermute | solution.py:27
  51.3 157.5 %all-gather.6.cloned.1.call-start = ((), (), s32[]{:S(2)}) async-start(), calls=%async_computation.3 | async-start | bytes 5734400 | tf_op jit(solution)/shard_map/all_gather | solution.py:447
  53.0 50.2 %collective-permute-start.11 = (bf16[128,2048]{1,0:T(8,128)(2,1)S(1)}, bf16[128,2048]{1,0:T(8,128)(2,1)}, u32[]{:S(2)}, u32[]{:S(2)}) collective-permute-start(bf16[128,2048]{1,0:T(8,128)(2,1)S(1)} %slice.753), channel_id=1, source_target_pairs={{0,2},{1,3},{2,0},{3,1},{4,6},{5,7},{6,4},{7,5},{8,10},{9,11},{10,... | collective-permute-start | bytes 1572872 | tf_op jit(solution)/shard_map/ppermute | solution.py:27
  90.0 40.3 %collective-permute-start.6 = (bf16[512,2336]{0,1:T(8,128)(2,1)}, bf16[512,2336]{0,1:T(8,128)(2,1)}, u32[]{:S(2)}, u32[]{:S(2)}) collective-permute-start(bf16[512,2336]{0,1:T(8,128)(2,1)} %copy.228), channel_id=1, source_target_pairs={{0,16},{16,0},{1,17},{17,1},{2,18},{18,2},{3,19},{19,3},{4,20},{20... | collective-permute-start | bytes 7176200 | tf_op jit(solution)/shard_map/ppermute | solution.py:22
  105.6 22.3 %collective-permute-start.12 = (bf16[2,128,2048]{2,1,0:T(8,128)(2,1)}, bf16[2,128,2048]{2,1,0:T(8,128)(2,1)}, u32[]{:S(2)}, u32[]{:S(2)}) collective-permute-start(bf16[2,128,2048]{2,1,0:T(8,128)(2,1)} %pad_maximum_fusion.9), channel_id=1, source_target_pairs={{0,1},{1,0},{2,3},{3,2},{4,5},{5,4},{6,7},{7,6},{8,9},{9,8},{10,11... | collective-permute-start | bytes 3145736 | tf_op jit(solution)/shard_map/ppermute | solution.py:27
  125.1 134.5 %all-gather.8.cloned.1.call-start = ((), (), s32[]{:S(2)}) async-start(), calls=%async_computation.4 | async-start | bytes 2621440 | tf_op jit(solution)/shard_map/all_gather | solution.py:447
  151.7 66.8 %collective-permute-start.13 = (bf16[512,2048]{1,0:T(8,128)(2,1)}, bf16[512,2048]{1,0:T(8,128)(2,1)}, u32[]{:S(2)}, u32[]{:S(2)}) collective-permute-start(bf16[512,2048]{1,0:T(8,128)(2,1)} %bitcast.28), channel_id=1, source_target_pairs={{0,16},{16,0},{1,17},{17,1},{2,18},{18,2},{3,19},{19,3},{4,20},{20... | collective-permute-start | bytes 6291464 | tf_op jit(solution)/shard_map/ppermute | solution.py:22
  158.2 27.6 %collective-permute-start.9 = (bf16[128,2048]{1,0:T(8,128)(2,1)}, bf16[128,2048]{1,0:T(8,128)(2,1)}, u32[]{:S(2)}, u32[]{:S(2)}) collective-permute-start(bf16[128,2048]{1,0:T(8,128)(2,1)} %add_convert_fusion.15), channel_id=1, source_target_pairs={{0,4},{4,8},{8,12},{1,5},{5,9},{9,13},{2,6},{6,10},{10,14},{3,7},{... | collective-permute-start | bytes 1572872 | tf_op jit(solution)/shard_map/ppermute | solution.py:18
  187.8 28.1 %collective-permute-start.10 = (bf16[128,2048]{1,0:T(8,128)(2,1)}, bf16[128,2048]{1,0:T(8,128)(2,1)S(1)}, u32[]{:S(2)}, u32[]{:S(2)}) collective-permute-start(bf16[128,2048]{1,0:T(8,128)(2,1)} %add_convert_fusion.14), channel_id=1, source_target_pairs={{0,4},{4,8},{8,12},{1,5},{5,9},{9,13},{2,6},{6,10},{10,14},{3,7},{... | collective-permute-start | bytes 1572872 | tf_op jit(solution)/shard_map/ppermute | solution.py:18
  194.3 33.2 %collective-permute-start.15 = (bf16[1024,1024]{1,0:T(8,128)(2,1)}, bf16[1024,1024]{1,0:T(8,128)(2,1)}, u32[]{:S(2)}, u32[]{:S(2)}) collective-permute-start(bf16[1024,1024]{1,0:T(8,128)(2,1)} %all-gather.4.cloned.1.call-done), channel_id=1, source_target_pairs={{0,16},{16,0},{1,17},{17,1},{2,18},{18,2},{3,19},{19,3},{4,20},{20... | collective-permute-start | bytes 6291464 | tf_op jit(solution)/shard_map/ppermute | solution.py:22
  215.4 47.9 %collective-permute-start.16 = (bf16[512,4384]{0,1:T(8,128)(2,1)}, bf16[512,4384]{0,1:T(8,128)(2,1)}, u32[]{:S(2)}, u32[]{:S(2)}) collective-permute-start(bf16[512,4384]{0,1:T(8,128)(2,1)} %copy.234), channel_id=1, source_target_pairs={{0,16},{16,0},{1,17},{17,1},{2,18},{18,2},{3,19},{19,3},{4,20},{20... | collective-permute-start | bytes 13467656 | tf_op jit(solution)/shard_map/ppermute | solution.py:22
  224.4 504.1 %reduce-scatter.5.cloned.1.call-start = ((), (), s32[]{:S(2)}) async-start(), calls=%async_computation.5 | async-start | bytes 2621440 | tf_op jit(solution)/shard_map/reduce_scatter | solution.py:388
  259.6 46.3 %collective-permute-start.21 = (bf16[1024,1024]{1,0:T(8,128)(2,1)}, bf16[1024,1024]{1,0:T(8,128)(2,1)}, u32[]{:S(2)}, u32[]{:S(2)}) collective-permute-start(bf16[1024,1024]{1,0:T(8,128)(2,1)} %all-gather.8.cloned.1.call-done), channel_id=1, source_target_pairs={{0,16},{16,0},{1,17},{17,1},{2,18},{18,2},{3,19},{19,3},{4,20},{20... | collective-permute-start | bytes 6291464 | tf_op jit(solution)/shard_map/ppermute | solution.py:22
  283.1 18.7 %collective-permute-start.18 = (bf16[128,2048]{1,0:T(8,128)(2,1)}, bf16[128,2048]{1,0:T(8,128)(2,1)}, u32[]{:S(2)}, u32[]{:S(2)}) collective-permute-start(bf16[128,2048]{1,0:T(8,128)(2,1)} %get-tuple-element.259), channel_id=1, source_target_pairs={{0,4},{4,8},{8,12},{1,5},{5,9},{9,13},{2,6},{6,10},{10,14},{3,7},{... | collective-permute-start | bytes 1572872 | tf_op jit(solution)/shard_map/ppermute | solution.py:18
  303.2 13.8 %collective-permute-start.19 = (bf16[128,2048]{1,0:T(8,128)(2,1)S(1)}, bf16[128,2048]{1,0:T(8,128)(2,1)S(1)}, u32[]{:S(2)}, u32[]{:S(2)}) collective-permute-start(bf16[128,2048]{1,0:T(8,128)(2,1)S(1)} %add_convert_fusion.13), channel_id=1, source_target_pairs={{0,4},{4,8},{8,12},{1,5},{5,9},{9,13},{2,6},{6,10},{10,14},{3,7},{... | collective-permute-start | bytes 1572872 | tf_op jit(solution)/shard_map/ppermute | solution.py:18
  317.2 14.8 %collective-permute-start.20 = (bf16[128,2048]{1,0:T(8,128)(2,1)S(1)}, bf16[128,2048]{1,0:T(8,128)(2,1)S(1)}, u32[]{:S(2)}, u32[]{:S(2)}) collective-permute-start(bf16[128,2048]{1,0:T(8,128)(2,1)S(1)} %add_convert_fusion.12), channel_id=1, source_target_pairs={{0,4},{4,8},{8,12},{1,5},{5,9},{9,13},{2,6},{6,10},{10,14},{3,7},{... | collective-permute-start | bytes 1572872 | tf_op jit(solution)/shard_map/ppermute | solution.py:18
  350.1 212.1 %collective-permute-start.22 = (bf16[256,1024]{1,0:T(8,128)(2,1)}, bf16[256,1024]{1,0:T(8,128)(2,1)}, u32[]{:S(2)}, u32[]{:S(2)}) collective-permute-start(bf16[256,1024]{1,0:T(8,128)(2,1)} %get-tuple-element.273), channel_id=1, source_target_pairs={{0,16},{16,0},{1,17},{17,1},{2,18},{18,2},{3,19},{19,3},{4,20},{20... | collective-permute-start | bytes 1572872 | tf_op jit(solution)/shard_map/ppermute | solution.py:22
  364.2 17.3 %collective-permute-start.23 = (bf16[128,2048]{1,0:T(8,128)(2,1)}, bf16[128,2048]{1,0:T(8,128)(2,1)}, u32[]{:S(2)}, u32[]{:S(2)}) collective-permute-start(bf16[128,2048]{1,0:T(8,128)(2,1)} %get-tuple-element.262), channel_id=1, source_target_pairs={{4,0},{8,4},{12,8},{5,1},{9,5},{13,9},{6,2},{10,6},{14,10},{7,3},{... | collective-permute-start | bytes 1572872 | tf_op jit(solution)/shard_map/ppermute | solution.py:18
  370.8 74.5 %collective-permute-start.27 = (bf16[1024,1024]{1,0:T(8,128)(2,1)}, bf16[1024,1024]{1,0:T(8,128)(2,1)}, u32[]{:S(2)}, u32[]{:S(2)}) collective-permute-start(bf16[1024,1024]{1,0:T(8,128)(2,1)} %convolution_convert_fusion.5), channel_id=1, source_target_pairs={{0,16},{16,0},{1,17},{17,1},{2,18},{18,2},{3,19},{19,3},{4,20},{20... | collective-permute-start | bytes 6291464 | tf_op jit(solution)/shard_map/ppermute | solution.py:22
  372.0 67.2 %collective-permute-start.28 = (bf16[512,2048]{1,0:T(8,128)(2,1)S(1)}, bf16[512,2048]{1,0:T(8,128)(2,1)S(1)}, u32[]{:S(2)}, u32[]{:S(2)}) collective-permute-start(bf16[512,2048]{1,0:T(8,128)(2,1)S(1)} %convolution_convert_fusion.3), channel_id=1, source_target_pairs={{0,16},{16,0},{1,17},{17,1},{2,18},{18,2},{3,19},{19,3},{4,20},{20... | collective-permute-start | bytes 6291464 | tf_op jit(solution)/shard_map/ppermute | solution.py:22
  382.7 15.6 %collective-permute-start.24 = (bf16[128,2048]{1,0:T(8,128)(2,1)S(1)}, bf16[128,2048]{1,0:T(8,128)(2,1)S(1)}, u32[]{:S(2)}, u32[]{:S(2)}) collective-permute-start(bf16[128,2048]{1,0:T(8,128)(2,1)S(1)} %add_convert_fusion.11), channel_id=1, source_target_pairs={{4,0},{8,4},{12,8},{5,1},{9,5},{13,9},{6,2},{10,6},{14,10},{7,3},{... | collective-permute-start | bytes 1572872 | tf_op jit(solution)/shard_map/ppermute | solution.py:18
  398.5 14.8 %collective-permute-start.25 = (bf16[128,2048]{1,0:T(8,128)(2,1)S(1)}, bf16[128,2048]{1,0:T(8,128)(2,1)S(1)}, u32[]{:S(2)}, u32[]{:S(2)}) collective-permute-start(bf16[128,2048]{1,0:T(8,128)(2,1)S(1)} %add_convert_fusion.10), channel_id=1, source_target_pairs={{4,0},{8,4},{12,8},{5,1},{9,5},{13,9},{6,2},{10,6},{14,10},{7,3},{... | collective-permute-start | bytes 1572872 | tf_op jit(solution)/shard_map/ppermute | solution.py:18
  436.9 12.6 %collective-permute-start.29 = (bf16[512,2336]{0,1:T(8,128)(2,1)}, bf16[512,2336]{0,1:T(8,128)(2,1)}, u32[]{:S(2)}, u32[]{:S(2)}) collective-permute-start(bf16[512,2336]{0,1:T(8,128)(2,1)} %convolution_convert_fusion.1), channel_id=1, source_target_pairs={{0,16},{16,0},{1,17},{17,1},{2,18},{18,2},{3,19},{19,3},{4,20},{20... | collective-permute-start | bytes 7176200 | tf_op jit(solution)/shard_map/ppermute | solution.py:22
  468.1 26.9 %collective-permute-start.30 = (bf16[128,2048]{1,0:T(8,128)(2,1)}, bf16[128,2048]{1,0:T(8,128)(2,1)}, u32[]{:S(2)}, u32[]{:S(2)}) collective-permute-start(bf16[128,2048]{1,0:T(8,128)(2,1)} %get-tuple-element.269), channel_id=1, source_target_pairs={{4,0},{8,4},{12,8},{5,1},{9,5},{13,9},{6,2},{10,6},{14,10},{7,3},{... | collective-permute-start | bytes 1572872 | tf_op jit(solution)/shard_map/ppermute | solution.py:18
  491.4 237.1 %reduce-scatter.7.cloned.1.call-start = ((), (), s32[]{:S(2)}) async-start(), calls=%async_computation.6 | async-start | bytes 5734400 | tf_op jit(solution)/shard_map/reduce_scatter | solution.py:388
  495.0 89.3 %collective-permute-start.38 = (bf16[1024,1024]{1,0:T(8,128)(2,1)}, bf16[1024,1024]{1,0:T(8,128)(2,1)}, u32[]{:S(2)}, u32[]{:S(2)}) collective-permute-start(bf16[1024,1024]{1,0:T(8,128)(2,1)} %convolution_convert_fusion.4), channel_id=1, source_target_pairs={{0,16},{16,0},{1,17},{17,1},{2,18},{18,2},{3,19},{19,3},{4,20},{20... | collective-permute-start | bytes 6291464 | tf_op jit(solution)/shard_map/ppermute | solution.py:22
  496.3 17.7 %collective-permute-start.31 = (bf16[128,2048]{1,0:T(8,128)(2,1)S(1)}, bf16[128,2048]{1,0:T(8,128)(2,1)S(1)}, u32[]{:S(2)}, u32[]{:S(2)}) collective-permute-start(bf16[128,2048]{1,0:T(8,128)(2,1)S(1)} %add_convert_fusion.9), channel_id=1, source_target_pairs={{4,0},{8,4},{12,8},{5,1},{9,5},{13,9},{6,2},{10,6},{14,10},{7,3},{... | collective-permute-start | bytes 1572872 | tf_op jit(solution)/shard_map/ppermute | solution.py:18
  499.7 89.0 %collective-permute-start.35 = (bf16[512,2048]{1,0:T(8,128)(2,1)}, bf16[512,2048]{1,0:T(8,128)(2,1)}, u32[]{:S(2)}, u32[]{:S(2)}) collective-permute-start(bf16[512,2048]{1,0:T(8,128)(2,1)} %convolution_convert_fusion.2), channel_id=1, source_target_pairs={{0,16},{16,0},{1,17},{17,1},{2,18},{18,2},{3,19},{19,3},{4,20},{20... | collective-permute-start | bytes 6291464 | tf_op jit(solution)/shard_map/ppermute | solution.py:22
  514.2 15.9 %collective-permute-start.32 = (bf16[128,2048]{1,0:T(8,128)(2,1)S(1)}, bf16[128,2048]{1,0:T(8,128)(2,1)S(1)}, u32[]{:S(2)}, u32[]{:S(2)}) collective-permute-start(bf16[128,2048]{1,0:T(8,128)(2,1)S(1)} %add_convert_fusion.8), channel_id=1, source_target_pairs={{4,0},{8,4},{12,8},{5,1},{9,5},{13,9},{6,2},{10,6},{14,10},{7,3},{... | collective-permute-start | bytes 1572872 | tf_op jit(solution)/shard_map/ppermute | solution.py:18
  572.7 227.3 %all-reduce.3.cloned.1.call-start = ((), (), s32[]{:S(2)}) async-start(), calls=%async_computation.7 | async-start | bytes 3342336 | tf_op jit(solution)/shard_map/psum | solution.py:388
  581.5 14.3 %collective-permute-start.62 = (f32[14688]{0:T(1024)S(1)}, f32[14688]{0:T(1024)S(1)}, u32[]{:S(2)}, u32[]{:S(2)}) collective-permute-start(f32[14688]{0:T(1024)S(1)} %add.571), channel_id=1, source_target_pairs={{0,8},{4,12},{8,0},{12,4},{1,9},{5,13},{9,1},{13,5},{2,10},{6,14},... | collective-permute-start | bytes 176264 | tf_op jit(solution)/shard_map/ppermute | solution.py:27
  588.4 39.6 %collective-permute-start.39 = (bf16[2,256,1024]{2,1,0:T(8,128)(2,1)}, bf16[2,256,1024]{2,1,0:T(8,128)(2,1)}, u32[]{:S(2)}, u32[]{:S(2)}) collective-permute-start(bf16[2,256,1024]{2,1,0:T(8,128)(2,1)} %bitcast.60), channel_id=1, source_target_pairs={{0,2},{1,3},{2,0},{3,1},{4,6},{5,7},{6,4},{7,5},{8,10},{9,11},{10,... | collective-permute-start | bytes 3145736 | tf_op jit(solution)/shard_map/ppermute | solution.py:27
  592.3 38.9 %collective-permute-start.36 = (bf16[2,128,2048]{2,1,0:T(8,128)(2,1)}, bf16[2,128,2048]{2,1,0:T(8,128)(2,1)}, u32[]{:S(2)}, u32[]{:S(2)}) collective-permute-start(bf16[2,128,2048]{2,1,0:T(8,128)(2,1)} %select_bitcast_fusion.4), channel_id=1, source_target_pairs={{0,1},{1,0},{2,3},{3,2},{4,5},{5,4},{6,7},{7,6},{8,9},{9,8},{10,11... | collective-permute-start | bytes 3145736 | tf_op jit(solution)/shard_map/ppermute | solution.py:27
  595.2 216.2 %collective-permute-start.34 = (bf16[256,1024]{1,0:T(8,128)(2,1)}, bf16[256,1024]{1,0:T(8,128)(2,1)}, u32[]{:S(2)}, u32[]{:S(2)}) collective-permute-start(bf16[256,1024]{1,0:T(8,128)(2,1)} %get-tuple-element.126), channel_id=1, source_target_pairs={{0,16},{16,0},{1,17},{17,1},{2,18},{18,2},{3,19},{19,3},{4,20},{20... | collective-permute-start | bytes 1572872 | tf_op jit(solution)/shard_map/ppermute | solution.py:22
  595.2 63.7 %collective-permute-start.45 = (bf16[512,2336]{0,1:T(8,128)(2,1)}, bf16[512,2336]{0,1:T(8,128)(2,1)}, u32[]{:S(2)}, u32[]{:S(2)}) collective-permute-start(bf16[512,2336]{0,1:T(8,128)(2,1)} %convolution_convert_fusion), channel_id=1, source_target_pairs={{0,16},{16,0},{1,17},{17,1},{2,18},{18,2},{3,19},{19,3},{4,20},{20... | collective-permute-start | bytes 7176200 | tf_op jit(solution)/shard_map/ppermute | solution.py:22
  629.6 24.2 %collective-permute-start.40 = (bf16[256,1024]{1,0:T(8,128)(2,1)S(1)}, bf16[256,1024]{1,0:T(8,128)(2,1)S(1)}, u32[]{:S(2)}, u32[]{:S(2)}) collective-permute-start(bf16[256,1024]{1,0:T(8,128)(2,1)S(1)} %select_bitcast_fusion.15), channel_id=1, source_target_pairs={{0,1},{1,0},{2,3},{3,2},{4,5},{5,4},{6,7},{7,6},{8,9},{9,8},{10,11... | collective-permute-start | bytes 1572872 | tf_op jit(solution)/shard_map/ppermute | solution.py:27
  633.0 23.2 %collective-permute-start.37 = (bf16[128,2048]{1,0:T(8,128)(2,1)S(1)}, bf16[128,2048]{1,0:T(8,128)(2,1)S(1)}, u32[]{:S(2)}, u32[]{:S(2)}) collective-permute-start(bf16[128,2048]{1,0:T(8,128)(2,1)S(1)} %select_bitcast_fusion.16), channel_id=1, source_target_pairs={{0,2},{1,3},{2,0},{3,1},{4,6},{5,7},{6,4},{7,5},{8,10},{9,11},{10,... | collective-permute-start | bytes 1572872 | tf_op jit(solution)/shard_map/ppermute | solution.py:27
  657.5 13.6 %collective-permute-start.41 = (bf16[2,32,4096]{2,1,0:T(8,128)(2,1)}, bf16[2,32,4096]{2,1,0:T(8,128)(2,1)}, u32[]{:S(2)}, u32[]{:S(2)}) collective-permute-start(bf16[2,32,4096]{2,1,0:T(8,128)(2,1)} %fusion.91), channel_id=1, source_target_pairs={{0,4},{4,0},{8,12},{12,8},{1,5},{5,1},{9,13},{13,9},{2,6},{6,2},{1... | collective-permute-start | bytes 1572872 | tf_op jit(solution)/shard_map/ppermute | solution.py:27
  663.6 25.5 %collective-permute-start.48 = (bf16[2,128,1184]{1,2,0:T(8,128)(2,1)}, bf16[2,128,1184]{1,2,0:T(8,128)(2,1)}, u32[]{:S(2)}, u32[]{:S(2)}) collective-permute-start(bf16[2,128,1184]{1,2,0:T(8,128)(2,1)} %bitcast.351), channel_id=1, source_target_pairs={{0,2},{1,3},{2,0},{3,1},{4,6},{5,7},{6,4},{7,5},{8,10},{9,11},{10,... | collective-permute-start | bytes 1818632 | tf_op jit(solution)/shard_map/ppermute | solution.py:27
  672.3 13.3 %collective-permute-start.42 = (bf16[32,4096]{1,0:T(8,128)(2,1)S(1)}, bf16[32,4096]{1,0:T(8,128)(2,1)S(1)}, u32[]{:S(2)}, u32[]{:S(2)}) collective-permute-start(bf16[32,4096]{1,0:T(8,128)(2,1)S(1)} %select_bitcast_fusion.29), channel_id=1, source_target_pairs={{0,8},{4,12},{8,0},{12,4},{1,9},{5,13},{9,1},{13,5},{2,10},{6,14},... | collective-permute-start | bytes 786440 | tf_op jit(solution)/shard_map/ppermute | solution.py:27
  674.9 13.5 %collective-permute-start.46 = (bf16[2,128,1152]{1,2,0:T(8,128)(2,1)S(1)}, bf16[2,128,1152]{1,2,0:T(8,128)(2,1)S(1)}, u32[]{:S(2)}, u32[]{:S(2)}) collective-permute-start(bf16[2,128,1152]{1,2,0:T(8,128)(2,1)S(1)} %select_bitcast_fusion.10), channel_id=1, source_target_pairs={{0,1},{1,0},{2,3},{3,2},{4,5},{5,4},{6,7},{7,6},{8,9},{9,8},{10,11... | collective-permute-start | bytes 1769480 | tf_op jit(solution)/shard_map/ppermute | solution.py:27
  685.7 14.9 %collective-permute-start.43 = (bf16[32,4096]{1,0:T(8,128)(2,1)S(1)}, bf16[32,4096]{1,0:T(8,128)(2,1)}, u32[]{:S(2)}, u32[]{:S(2)}) collective-permute-start(bf16[32,4096]{1,0:T(8,128)(2,1)S(1)} %fusion.93), channel_id=1, source_target_pairs={{0,8},{4,12},{8,0},{12,4},{1,9},{5,13},{9,1},{13,5},{2,10},{6,14},... | collective-permute-start | bytes 786440 | tf_op jit(solution)/shard_map/ppermute | solution.py:27
  706.9 17.9 %collective-permute-start.44 = (bf16[2,32,4096]{2,1,0:T(8,128)(2,1)S(1)}, bf16[2,32,4096]{2,1,0:T(8,128)(2,1)S(1)}, u32[]{:S(2)}, u32[]{:S(2)}) collective-permute-start(bf16[2,32,4096]{2,1,0:T(8,128)(2,1)S(1)} %pad_maximum_fusion.18), channel_id=1, source_target_pairs={{0,4},{4,0},{8,12},{12,8},{1,5},{5,1},{9,13},{13,9},{2,6},{6,2},{1... | collective-permute-start | bytes 1572872 | tf_op jit(solution)/shard_map/ppermute | solution.py:27
  733.9 79.8 %collective-permute-start.54 = (bf16[128,4384]{0,1:T(8,128)(2,1)}, bf16[128,4384]{0,1:T(8,128)(2,1)}, u32[]{:S(2)}, u32[]{:S(2)}) collective-permute-start(bf16[128,4384]{0,1:T(8,128)(2,1)} %copy.273), channel_id=1, source_target_pairs={{16,0},{17,1},{18,2},{19,3},{20,4},{21,5},{22,6},{23,7},{24,8},{25... | collective-permute-start | bytes 3366920 | tf_op jit(solution)/shard_map/ppermute | solution.py:417
  802.5 16.6 %collective-permute-start.55 = (bf16[128,4384]{0,1:T(8,128)(2,1)}, bf16[128,4384]{0,1:T(8,128)(2,1)}, u32[]{:S(2)}, u32[]{:S(2)}) collective-permute-start(bf16[128,4384]{0,1:T(8,128)(2,1)} %copy.274), channel_id=1, source_target_pairs={{0,16},{1,17},{2,18},{3,19},{4,20},{5,21},{6,22},{7,23},{8,24},{9,... | collective-permute-start | bytes 3366920 | tf_op jit(solution)/shard_map/ppermute | solution.py:418
  (215 other events, 1688.7 us)
Sparse Core Ops, SparseCore 0:
  51.5 51.5 all-gather.3
  125.2 56.4 all-gather.5
  224.5 35.0 all-gather.7
  491.5 38.0 reduce-scatter.4
  572.8 83.6 reduce-scatter.6
  728.7 71.3 all-reduce.2

commit v3 on v2

--- a/solution.py
+++ b/solution.py
@@ -384,11 +384,7 @@
     return (mine + swapped(other).astype(F32)).astype(BF16)
 
 
-def reduced_ahead(both):
-    return lax.psum(lax.psum_scatter(both, "wt", scatter_dimension=0, tiled=True), "seq")
-
-
-def reduced_last(gate, rest, out):
+def reduced(gate, rest, out):
     order = bits_of("wt")
     wide = LANES * (rest.shape[1] // (2 * LANES))
     gate = scatter_rows(gate, "wt", order)
@@ -472,7 +468,8 @@
         gather_rows(win_halves[0][:, inner:], "wt", order),
     )
     win0 = (win0_mine, tuple(swapped(part) for part in win0_mine))
-    wout0 = gathered(wout_halves[0])
+    next_half, _ = lax.optimization_barrier((wout_halves[0], win0_mine))
+    wout0 = gathered(next_half)
     next_half, _ = lax.optimization_barrier((win_halves[1], wout0[0]))
     win1 = gathered(next_half)
     next_half, _ = lax.optimization_barrier((wout_halves[1], win1[0]))
@@ -487,14 +484,13 @@
     back1, gwin1, gwout1, gsmall1 = layer_backward(
         own_cotangent, saved1, weights[1], smalls[1], first, parts
     )
-    both_wout1 = both_cores(gwout1)
-    both_win1 = jnp.concatenate([both_cores(part) for part in gwin1], axis=1)
-    back1, both_wout1, both_win1 = lax.optimization_barrier((back1, both_wout1, both_win1))
-    sum_wout1, sum_win1 = reduced_ahead(both_wout1), reduced_ahead(both_win1)
+    both1 = (both_cores(gwin1[0]), both_cores(gwin1[1]), both_cores(gwout1))
+    back1, both1 = lax.optimization_barrier((back1, both1))
+    sum_win1, sum_wout1 = reduced(*both1)
     back0, gwin0, gwout0, gsmall0 = layer_backward(
         back1, saved0, weights[0], smalls[0], first, parts
     )
-    sum_win0, sum_wout0 = reduced_last(
+    sum_win0, sum_wout0 = reduced(
         both_cores(gwin0[0]), both_cores(gwin0[1]), both_cores(gwout0)
     )
     input_grads = by_layer((back0, back1), first)

time: 851 us -> 863 us (1.014)
  waiting for transfers between devices: 324 us -> 289 us
  other arithmetic: 92.9 us -> 115 us
  starting transfers between devices: 89.8 us -> 102 us
    psum x1 -> x0, waiting for transfers between devices: 60.5 us -> none  [reduced_ahead(): lax.psum(lax.psum_scatter(both, 'wt', scatter_dimension=0, tiled=True), '...]
    ppermute x27 -> x43, waiting for transfers between devices: 157 us -> 185 us  [crossed(): return lax.ppermute(block, axis, [(i, i ^ bit) for i in devices])]
    ppermute x16, waiting for transfers between devices: 84.6 us -> 69.4 us  [shifted(): return lax.ppermute(block, axis, route)]
    ppermute x27 -> x43, starting transfers between devices: 36.2 us -> 50.6 us  [crossed(): return lax.ppermute(block, axis, [(i, i ^ bit) for i in devices])]
    all_gather x3, waiting for transfers between devices: 21.5 us -> 33.6 us  [gathered(): mine = lax.all_gather(half, 'wt', axis=0, tiled=True)]
    unnamed x424 -> x527, local copies, waits for them, and re-layouts: 33.2 us -> 36 us
  transfers between devices with their start and end apart: 69 -> 82, of which waited for: 30 -> 36; matrix products, arithmetic and copies ran while one was open for 37% -> 36% of each run, Pallas kernels for 6% -> 5%
where the time goes in v3:
time: 863 us; the launch traced here: 848 us
  waiting for transfers between devices  289 us (33%)
  local copies, waits for them, and re-layouts  138 us (16%)
  matrix products  133 us (15%)
  other arithmetic  115 us (13%)
  starting transfers between devices  102 us (12%)
  Pallas kernels  52.6 us (6%)
  between operations  18.7 us (2%)
    ppermute x43, waiting for transfers between devices, crossed(): return lax.ppermute(block, axis, [(i, i ^ bit) for i in devices])  185 us
    dot_general x58, matrix products, dot(): lax.dot_general(a.astype(BF16), b.astype(BF16), (over, ((), ())), preferr...  114 us
    ppermute x16, waiting for transfers between devices, shifted(): return lax.ppermute(block, axis, route)  69.4 us
    ppermute x43, starting transfers between devices, crossed(): return lax.ppermute(block, axis, [(i, i ^ bit) for i in devices])  50.6 us
    ppermute x16, starting transfers between devices, shifted(): return lax.ppermute(block, axis, route)  41.5 us
    unnamed x527, local copies, waits for them, and re-layouts  36 us
    all_gather x3, waiting for transfers between devices, gathered(): mine = lax.all_gather(half, 'wt', axis=0, tiled=True)  33.6 us
    pallas_call x2, Pallas kernels, within_back(): pl.pallas_call(lambda *refs: within_back_kernel(head_size, *refs), grid=(...  28.5 us
  transfers between devices with their start and end apart: 82, of which 36 were waited for; matrix products, arithmetic and copies ran while one was open for 36% of the time, Pallas kernels for 5%

profile of v3, /device:TPU:0, one launch (start us, length us, event | category | flops | bytes accessed | tf_op | source)
XLA Modules:
  0.0 848.0 jit_solution(2291908368525221708)
XLA Ops:
  21.8 11.2 %collective-permute-done.11 = bf16[128,2048]{1,0:T(8,128)(2,1)} collective-permute-done((bf16[128,2048]{1,0:T(8,128)(2,1)S(1)}, bf16[128,2048]{1,0:T(8,128)(2,1)}, u32[]{:S(2)}, u32[]{:S(2)}) %collective-permute-start.11) | collective-permute-done | bytes 524320 | tf_op jit(solution)/shard_map/ppermute | solution.py:27
  46.0 13.2 %collective-permute-done.12 = bf16[2,128,2048]{2,1,0:T(8,128)(2,1)} collective-permute-done((bf16[2,128,2048]{2,1,0:T(8,128)(2,1)}, bf16[2,128,2048]{2,1,0:T(8,128)(2,1)}, u32[]{:S(2)}, u32[]{:S(2)}) %collective-permute-start.12) | collective-permute-done | bytes 1048608 | tf_op jit(solution)/shard_map/ppermute | solution.py:27
  62.2 6.8 collective-permute-done.5
  94.9 14.5 %all-gather.4.cloned.1.call-done = bf16[1024,1024]{1,0:T(8,128)(2,1)} async-done(((bf16[256,1024]{1,0:T(8,128)(2,1)}), bf16[1024,1024]{1,0:T(8,128)(2,1)}) %all-gather.4.cloned.1.call-update) | async-done | bytes 2097168 | tf_op jit(solution)/shard_map/all_gather | solution.py:443
  113.6 3.6 collective-permute-start.7
  132.5 8.4 collective-permute-done.8
  141.8 5.2 collective-permute-start.9
  174.4 3.7 fusion.266
  180.5 12.1 %shard_map.194 = f32[256,2048]{1,0:T(8,128)} custom-call(f32[256,2048]{1,0:T(8,128)} %get-tuple-element.139.refs_0_, f32[256,32]{1,0:T(8,128)} %copy.287.refs_1_.refs_2_, f32[32,256]{1,0:T(8,128)} %bitcast.504, f32[256,128]{1,0:T(8,128)} %get-tuple-element.156.refs_3_.refs_4_, f32[256,128]{1,0:T(8,128)} %get-tuple-element.155.refs_4_.refs_5_), custom_call_target="tpu_custom_call" | custom-call | flops 1073741824 | bytes 4194304 | tf_op jit(solution)/shard_map/pallas_call | solution.py:175
  192.6 6.5 copy.290
  202.4 5.7 multiply_reduce_fusion.15
  221.8 19.1 %all-gather.8.cloned.1.call-done = bf16[1024,1024]{1,0:T(8,128)(2,1)} async-done(((bf16[256,1024]{1,0:T(8,128)(2,1)}), bf16[1024,1024]{1,0:T(8,128)(2,1)}) %all-gather.8.cloned.1.call-update) | async-done | bytes 2097168 | tf_op jit(solution)/shard_map/all_gather | solution.py:443
  240.9 3.6 fusion.109
  247.2 3.9 collective-permute-start.17
  264.9 4.2 collective-permute-start.18
  271.6 12.1 %shard_map.195 = f32[256,2048]{1,0:T(8,128)} custom-call(f32[256,2048]{1,0:T(8,128)} %get-tuple-element.133.refs_0_, f32[256,32]{1,0:T(8,128)} %copy.293.refs_1_.refs_2_, f32[32,256]{1,0:T(8,128)} %bitcast.506, f32[256,128]{1,0:T(8,128)} %get-tuple-element.154.refs_3_.refs_4_, f32[256,128]{1,0:T(8,128)} %get-tuple-element.153.refs_4_.refs_5_), custom_call_target="tpu_custom_call" | custom-call | flops 1073741824 | bytes 4194304 | tf_op jit(solution)/shard_map/pallas_call | solution.py:175
  290.2 8.6 %collective-permute-done.19 = bf16[128,2048]{1,0:T(8,128)(2,1)S(1)} collective-permute-done((bf16[128,2048]{1,0:T(8,128)(2,1)S(1)}, bf16[128,2048]{1,0:T(8,128)(2,1)S(1)}, u32[]{:S(2)}, u32[]{:S(2)}) %collective-permute-start.19) | collective-permute-done | bytes 524320 | tf_op jit(solution)/shard_map/ppermute | solution.py:18
  299.0 4.6 collective-permute-start.20
  303.7 10.0 %collective-permute-done.20 = bf16[128,2048]{1,0:T(8,128)(2,1)S(1)} collective-permute-done((bf16[128,2048]{1,0:T(8,128)(2,1)S(1)}, bf16[128,2048]{1,0:T(8,128)(2,1)S(1)}, u32[]{:S(2)}, u32[]{:S(2)}) %collective-permute-start.20) | collective-permute-done | bytes 524320 | tf_op jit(solution)/shard_map/ppermute | solution.py:18
  315.0 3.6 multiply_reduce_fusion.14
  333.7 14.2 %shard_map.196 = (f32[256,2048]{1,0:T(8,128)}, f32[256,256]{1,0:T(8,128)}, f32[256,32]{1,0:T(8,128)}, f32[32,256]{1,0:T(8,128)}) custom-call(f32[256,2048]{1,0:T(8,128)} %get-tuple-element.133.refs_0_, f32[256,2048]{1,0:T(8,128)} %convert_element_type.683.refs_1_, f32[256,32]{1,0:T(8,128)} %copy.293.refs_1_.refs_2_, f32[32,256]{1,0:T(8,128)} %bitcast.507, ...), custom_call_target="tpu_custom_call" | custom-call | flops 2147483648 | bytes 6291456 | tf_op jit(solution)/shard_map/pallas_call | solution.py:194
  350.7 3.6 convolution_convert_fusion.3
  358.2 6.8 collective-permute-done.23
  368.3 13.6 %collective-permute-done.24 = bf16[128,2048]{1,0:T(8,128)(2,1)S(1)} collective-permute-done((bf16[128,2048]{1,0:T(8,128)(2,1)S(1)}, bf16[128,2048]{1,0:T(8,128)(2,1)S(1)}, u32[]{:S(2)}, u32[]{:S(2)}) %collective-permute-start.24) | collective-permute-done | bytes 524320 | tf_op jit(solution)/shard_map/ppermute | solution.py:18
  387.0 10.0 %collective-permute-done.25 = bf16[128,2048]{1,0:T(8,128)(2,1)S(1)} collective-permute-done((bf16[128,2048]{1,0:T(8,128)(2,1)S(1)}, bf16[128,2048]{1,0:T(8,128)(2,1)S(1)}, u32[]{:S(2)}, u32[]{:S(2)}) %collective-permute-start.25) | collective-permute-done | bytes 524320 | tf_op jit(solution)/shard_map/ppermute | solution.py:18
  414.0 4.8 fusion.15
  433.4 3.9 add_convert_fusion.5
  437.4 3.8 add_convert_fusion.4
  462.1 14.3 %shard_map.197 = (f32[256,2048]{1,0:T(8,128)}, f32[256,256]{1,0:T(8,128)}, f32[256,32]{1,0:T(8,128)}, f32[32,256]{1,0:T(8,128)}) custom-call(f32[256,2048]{1,0:T(8,128)} %get-tuple-element.139.refs_0_, f32[256,2048]{1,0:T(8,128)} %convert_element_type.714.refs_1_, f32[256,32]{1,0:T(8,128)} %copy.287.refs_1_.refs_2_, f32[32,256]{1,0:T(8,128)} %bitcast.505, ...), custom_call_target="tpu_custom_call" | custom-call | flops 2147483648 | bytes 6291456 | tf_op jit(solution)/shard_map/pallas_call | solution.py:194
  481.2 3.5 convolution_convert_fusion.2
  516.3 20.8 %collective-permute-done.63 = bf16[128,1152]{0,1:T(8,128)(2,1)S(1)} collective-permute-done((bf16[128,1152]{0,1:T(8,128)(2,1)S(1)}, bf16[128,1152]{0,1:T(8,128)(2,1)S(1)}, u32[]{:S(2)}, u32[]{:S(2)}) %collective-permute-start.63) | collective-permute-done | bytes 294944 | tf_op jit(solution)/shard_map/ppermute | solution.py:27
  538.5 6.4 collective-permute-done.65
  550.6 9.2 %collective-permute-done.31 = bf16[128,2048]{1,0:T(8,128)(2,1)} collective-permute-done((bf16[128,2048]{1,0:T(8,128)(2,1)}, bf16[128,2048]{1,0:T(8,128)(2,1)}, u32[]{:S(2)}, u32[]{:S(2)}) %collective-permute-start.31) | collective-permute-done | bytes 524320 | tf_op jit(solution)/shard_map/ppermute | solution.py:18
  576.1 9.3 %collective-permute-done.67 = bf16[32,2336]{1,0:T(8,128)(2,1)S(1)} collective-permute-done((bf16[32,2336]{1,0:T(8,128)(2,1)S(1)}, bf16[32,2336]{1,0:T(8,128)(2,1)S(1)}, u32[]{:S(2)}, u32[]{:S(2)}) %collective-permute-start.67) | collective-permute-done | bytes 149536 | tf_op jit(solution)/shard_map/ppermute | solution.py:27
  585.7 6.9 collective-permute-done.68
  613.4 5.0 fusion.7
  666.7 11.6 %collective-permute-done.59 = bf16[32,4096]{1,0:T(8,128)(2,1)S(1)} collective-permute-done((bf16[32,4096]{1,0:T(8,128)(2,1)S(1)}, bf16[32,4096]{1,0:T(8,128)(2,1)S(1)}, u32[]{:S(2)}, u32[]{:S(2)}) %collective-permute-start.59) | collective-permute-done | bytes 262176 | tf_op jit(solution)/shard_map/ppermute | solution.py:27
  680.1 12.5 %collective-permute-done.60 = bf16[32,4096]{1,0:T(8,128)(2,1)S(1)} collective-permute-done((bf16[32,4096]{1,0:T(8,128)(2,1)S(1)}, bf16[32,4096]{1,0:T(8,128)(2,1)S(1)}, u32[]{:S(2)}, u32[]{:S(2)}) %collective-permute-start.60) | collective-permute-done | bytes 262176 | tf_op jit(solution)/shard_map/ppermute | solution.py:27
  695.4 9.3 %collective-permute-done.36 = bf16[2,128,2048]{2,1,0:T(8,128)(2,1)S(1)} collective-permute-done((bf16[2,128,2048]{2,1,0:T(8,128)(2,1)S(1)}, bf16[2,128,2048]{2,1,0:T(8,128)(2,1)S(1)}, u32[]{:S(2)}, u32[]{:S(2)}) %collective-permute-start.36) | collective-permute-done | bytes 1048608 | tf_op jit(solution)/shard_map/ppermute | solution.py:27
  738.5 9.6 %collective-permute-done.42 = bf16[32,4096]{1,0:T(8,128)(2,1)S(1)} collective-permute-done((bf16[32,4096]{1,0:T(8,128)(2,1)S(1)}, bf16[32,4096]{1,0:T(8,128)(2,1)S(1)}, u32[]{:S(2)}, u32[]{:S(2)}) %collective-permute-start.42) | collective-permute-done | bytes 262176 | tf_op jit(solution)/shard_map/ppermute | solution.py:27
  749.1 12.1 %collective-permute-done.46 = bf16[2,128,1152]{1,2,0:T(8,128)(2,1)S(1)} collective-permute-done((bf16[2,128,1152]{1,2,0:T(8,128)(2,1)S(1)}, bf16[2,128,1152]{1,2,0:T(8,128)(2,1)S(1)}, u32[]{:S(2)}, u32[]{:S(2)}) %collective-permute-start.46) | collective-permute-done | bytes 589856 | tf_op jit(solution)/shard_map/ppermute | solution.py:27
  763.2 5.1 collective-permute-done.47
  768.7 6.4 collective-permute-done.49
  777.8 7.3 collective-permute-done.50
  785.3 4.5 collective-permute-start.51
  796.1 8.9 %collective-permute-done.44 = bf16[2,32,4096]{2,1,0:T(8,128)(2,1)S(1)} collective-permute-done((bf16[2,32,4096]{2,1,0:T(8,128)(2,1)S(1)}, bf16[2,32,4096]{2,1,0:T(8,128)(2,1)S(1)}, u32[]{:S(2)}, u32[]{:S(2)}) %collective-permute-start.44) | collective-permute-done | bytes 524320 | tf_op jit(solution)/shard_map/ppermute | solution.py:27
  806.5 5.6 collective-permute-done.53
  835.2 5.9 copy.348
  (998 shorter events, 433.7 us)
Async XLA Ops:
  7.2 102.2 %all-gather.4.cloned.1.call-start = ((), (), s32[]{:S(2)}) async-start(), calls=%async_computation | async-start | bytes 2621440 | tf_op jit(solution)/shard_map/all_gather | solution.py:443
  11.4 32.3 %collective-permute-start.14 = (bf16[256,1024]{1,0:T(8,128)(2,1)}, bf16[256,1024]{1,0:T(8,128)(2,1)}, u32[]{:S(2)}, u32[]{:S(2)}) collective-permute-start(bf16[256,1024]{1,0:T(8,128)(2,1)} %dynamic-slice_bitcast_fusion.1), channel_id=1, source_target_pairs={{0,16},{16,0},{1,17},{17,1},{2,18},{18,2},{3,19},{19,3},{4,20},{20... | collective-permute-start | bytes 1572872 | tf_op jit(solution)/shard_map/ppermute | solution.py:22
  20.7 22.9 %collective-permute-start.1 = (bf16[2,1,3672]{2,0,1:T(2,128)(2,1)S(1)}, bf16[2,1,3672]{2,0,1:T(2,128)(2,1)S(1)}, u32[]{:S(2)}, u32[]{:S(2)}) collective-permute-start(bf16[2,1,3672]{2,0,1:T(2,128)(2,1)S(1)} %pad_maximum_fusion.35), channel_id=1, source_target_pairs={{0,2},{1,3},{2,0},{3,1},{4,6},{5,7},{6,4},{7,5},{8,10},{9,11},{10,... | collective-permute-start | bytes 44072 | tf_op jit(solution)/shard_map/ppermute | solution.py:27
  35.1 24.1 %collective-permute-start.12 = (bf16[2,128,2048]{2,1,0:T(8,128)(2,1)}, bf16[2,128,2048]{2,1,0:T(8,128)(2,1)}, u32[]{:S(2)}, u32[]{:S(2)}) collective-permute-start(bf16[2,128,2048]{2,1,0:T(8,128)(2,1)} %pad_maximum_fusion.9), channel_id=1, source_target_pairs={{0,1},{1,0},{2,3},{3,2},{4,5},{5,4},{6,7},{7,6},{8,9},{9,8},{10,11... | collective-permute-start | bytes 3145736 | tf_op jit(solution)/shard_map/ppermute | solution.py:27
  42.1 26.8 %collective-permute-start.5 = (bf16[2,128,2336]{1,2,0:T(8,128)(2,1)}, bf16[2,128,2336]{1,2,0:T(8,128)(2,1)}, u32[]{:S(2)}, u32[]{:S(2)}) collective-permute-start(bf16[2,128,2336]{1,2,0:T(8,128)(2,1)} %copy.281), channel_id=1, source_target_pairs={{0,2},{1,3},{2,0},{3,1},{4,6},{5,7},{6,4},{7,5},{8,10},{9,11},{10,... | collective-permute-start | bytes 3588104 | tf_op jit(solution)/shard_map/ppermute | solution.py:27
  73.2 119.4 %all-gather.6.cloned.1.call-start = ((), (), s32[]{:S(2)}) async-start(), calls=%async_computation.1 | async-start | bytes 5734400 | tf_op jit(solution)/shard_map/all_gather | solution.py:443
  77.8 33.0 %collective-permute-start.6 = (bf16[512,2336]{0,1:T(8,128)(2,1)}, bf16[512,2336]{0,1:T(8,128)(2,1)}, u32[]{:S(2)}, u32[]{:S(2)}) collective-permute-start(bf16[512,2336]{0,1:T(8,128)(2,1)} %copy.284), channel_id=1, source_target_pairs={{0,16},{16,0},{1,17},{17,1},{2,18},{18,2},{3,19},{19,3},{4,20},{20... | collective-permute-start | bytes 7176200 | tf_op jit(solution)/shard_map/ppermute | solution.py:22
  109.4 131.5 %all-gather.8.cloned.1.call-start = ((), (), s32[]{:S(2)}) async-start(), calls=%async_computation.2 | async-start | bytes 2621440 | tf_op jit(solution)/shard_map/all_gather | solution.py:443
  130.0 72.3 %collective-permute-start.13 = (bf16[512,2048]{1,0:T(8,128)(2,1)}, bf16[512,2048]{1,0:T(8,128)(2,1)}, u32[]{:S(2)}, u32[]{:S(2)}) collective-permute-start(bf16[512,2048]{1,0:T(8,128)(2,1)} %bitcast.28), channel_id=1, source_target_pairs={{0,16},{16,0},{1,17},{17,1},{2,18},{18,2},{3,19},{19,3},{4,20},{20... | collective-permute-start | bytes 6291464 | tf_op jit(solution)/shard_map/ppermute | solution.py:22
  141.8 27.6 %collective-permute-start.9 = (bf16[128,2048]{1,0:T(8,128)(2,1)}, bf16[128,2048]{1,0:T(8,128)(2,1)}, u32[]{:S(2)}, u32[]{:S(2)}) collective-permute-start(bf16[128,2048]{1,0:T(8,128)(2,1)} %add_convert_fusion.15), channel_id=1, source_target_pairs={{0,4},{4,8},{8,12},{1,5},{5,9},{9,13},{2,6},{6,10},{10,14},{3,7},{... | collective-permute-start | bytes 1572872 | tf_op jit(solution)/shard_map/ppermute | solution.py:18
  171.5 28.2 %collective-permute-start.10 = (bf16[128,2048]{1,0:T(8,128)(2,1)}, bf16[128,2048]{1,0:T(8,128)(2,1)S(1)}, u32[]{:S(2)}, u32[]{:S(2)}) collective-permute-start(bf16[128,2048]{1,0:T(8,128)(2,1)} %add_convert_fusion.14), channel_id=1, source_target_pairs={{0,4},{4,8},{8,12},{1,5},{5,9},{9,13},{2,6},{6,10},{10,14},{3,7},{... | collective-permute-start | bytes 1572872 | tf_op jit(solution)/shard_map/ppermute | solution.py:18
  192.6 20.9 %collective-permute-start.15 = (bf16[1024,1024]{1,0:T(8,128)(2,1)}, bf16[1024,1024]{1,0:T(8,128)(2,1)}, u32[]{:S(2)}, u32[]{:S(2)}) collective-permute-start(bf16[1024,1024]{1,0:T(8,128)(2,1)} %all-gather.4.cloned.1.call-done), channel_id=1, source_target_pairs={{0,16},{16,0},{1,17},{17,1},{2,18},{18,2},{3,19},{19,3},{4,20},{20... | collective-permute-start | bytes 6291464 | tf_op jit(solution)/shard_map/ppermute | solution.py:22
  199.2 45.4 %collective-permute-start.16 = (bf16[512,4384]{0,1:T(8,128)(2,1)}, bf16[512,4384]{0,1:T(8,128)(2,1)}, u32[]{:S(2)}, u32[]{:S(2)}) collective-permute-start(bf16[512,4384]{0,1:T(8,128)(2,1)} %copy.290), channel_id=1, source_target_pairs={{0,16},{16,0},{1,17},{17,1},{2,18},{18,2},{3,19},{19,3},{4,20},{20... | collective-permute-start | bytes 13467656 | tf_op jit(solution)/shard_map/ppermute | solution.py:22
  240.9 46.7 %collective-permute-start.21 = (bf16[1024,1024]{1,0:T(8,128)(2,1)}, bf16[1024,1024]{1,0:T(8,128)(2,1)}, u32[]{:S(2)}, u32[]{:S(2)}) collective-permute-start(bf16[1024,1024]{1,0:T(8,128)(2,1)} %all-gather.8.cloned.1.call-done), channel_id=1, source_target_pairs={{0,16},{16,0},{1,17},{17,1},{2,18},{18,2},{3,19},{19,3},{4,20},{20... | collective-permute-start | bytes 6291464 | tf_op jit(solution)/shard_map/ppermute | solution.py:22
  264.9 18.8 %collective-permute-start.18 = (bf16[128,2048]{1,0:T(8,128)(2,1)}, bf16[128,2048]{1,0:T(8,128)(2,1)}, u32[]{:S(2)}, u32[]{:S(2)}) collective-permute-start(bf16[128,2048]{1,0:T(8,128)(2,1)} %get-tuple-element.279), channel_id=1, source_target_pairs={{0,4},{4,8},{8,12},{1,5},{5,9},{9,13},{2,6},{6,10},{10,14},{3,7},{... | collective-permute-start | bytes 1572872 | tf_op jit(solution)/shard_map/ppermute | solution.py:18
  333.7 50.9 %collective-permute-start.22 = (bf16[256,1024]{1,0:T(8,128)(2,1)}, bf16[256,1024]{1,0:T(8,128)(2,1)}, u32[]{:S(2)}, u32[]{:S(2)}) collective-permute-start(bf16[256,1024]{1,0:T(8,128)(2,1)} %get-tuple-element.293), channel_id=1, source_target_pairs={{0,16},{16,0},{1,17},{17,1},{2,18},{18,2},{3,19},{19,3},{4,20},{20... | collective-permute-start | bytes 1572872 | tf_op jit(solution)/shard_map/ppermute | solution.py:22
  347.8 17.3 %collective-permute-start.23 = (bf16[128,2048]{1,0:T(8,128)(2,1)}, bf16[128,2048]{1,0:T(8,128)(2,1)}, u32[]{:S(2)}, u32[]{:S(2)}) collective-permute-start(bf16[128,2048]{1,0:T(8,128)(2,1)} %get-tuple-element.282), channel_id=1, source_target_pairs={{4,0},{8,4},{12,8},{5,1},{9,5},{13,9},{6,2},{10,6},{14,10},{7,3},{... | collective-permute-start | bytes 1572872 | tf_op jit(solution)/shard_map/ppermute | solution.py:18
  354.3 79.1 %collective-permute-start.27 = (bf16[512,2048]{1,0:T(8,128)(2,1)}, bf16[512,2048]{1,0:T(8,128)(2,1)}, u32[]{:S(2)}, u32[]{:S(2)}) collective-permute-start(bf16[512,2048]{1,0:T(8,128)(2,1)} %convolution_convert_fusion.3), channel_id=1, source_target_pairs={{0,16},{16,0},{1,17},{17,1},{2,18},{18,2},{3,19},{19,3},{4,20},{20... | collective-permute-start | bytes 6291464 | tf_op jit(solution)/shard_map/ppermute | solution.py:22
  354.7 82.6 %collective-permute-start.29 = (bf16[1024,1024]{1,0:T(8,128)(2,1)}, bf16[1024,1024]{1,0:T(8,128)(2,1)}, u32[]{:S(2)}, u32[]{:S(2)}) collective-permute-start(bf16[1024,1024]{1,0:T(8,128)(2,1)} %convolution_convert_fusion.5), channel_id=1, source_target_pairs={{0,16},{16,0},{1,17},{17,1},{2,18},{18,2},{3,19},{19,3},{4,20},{20... | collective-permute-start | bytes 6291464 | tf_op jit(solution)/shard_map/ppermute | solution.py:22
  366.3 15.6 %collective-permute-start.24 = (bf16[128,2048]{1,0:T(8,128)(2,1)S(1)}, bf16[128,2048]{1,0:T(8,128)(2,1)S(1)}, u32[]{:S(2)}, u32[]{:S(2)}) collective-permute-start(bf16[128,2048]{1,0:T(8,128)(2,1)S(1)} %add_convert_fusion.11), channel_id=1, source_target_pairs={{4,0},{8,4},{12,8},{5,1},{9,5},{13,9},{6,2},{10,6},{14,10},{7,3},{... | collective-permute-start | bytes 1572872 | tf_op jit(solution)/shard_map/ppermute | solution.py:18
  382.1 14.9 %collective-permute-start.25 = (bf16[128,2048]{1,0:T(8,128)(2,1)S(1)}, bf16[128,2048]{1,0:T(8,128)(2,1)S(1)}, u32[]{:S(2)}, u32[]{:S(2)}) collective-permute-start(bf16[128,2048]{1,0:T(8,128)(2,1)S(1)} %add_convert_fusion.10), channel_id=1, source_target_pairs={{4,0},{8,4},{12,8},{5,1},{9,5},{13,9},{6,2},{10,6},{14,10},{7,3},{... | collective-permute-start | bytes 1572872 | tf_op jit(solution)/shard_map/ppermute | solution.py:18
  476.5 29.5 %collective-permute-start.30 = (bf16[128,2048]{1,0:T(8,128)(2,1)}, bf16[128,2048]{1,0:T(8,128)(2,1)}, u32[]{:S(2)}, u32[]{:S(2)}) collective-permute-start(bf16[128,2048]{1,0:T(8,128)(2,1)} %get-tuple-element.289), channel_id=1, source_target_pairs={{4,0},{8,4},{12,8},{5,1},{9,5},{13,9},{6,2},{10,6},{14,10},{7,3},{... | collective-permute-start | bytes 1572872 | tf_op jit(solution)/shard_map/ppermute | solution.py:18
  481.2 176.8 %collective-permute-start.38 = (bf16[1024,1024]{1,0:T(8,128)(2,1)}, bf16[1024,1024]{1,0:T(8,128)(2,1)}, u32[]{:S(2)}, u32[]{:S(2)}) collective-permute-start(bf16[1024,1024]{1,0:T(8,128)(2,1)} %convolution_convert_fusion.4), channel_id=1, source_target_pairs={{0,16},{16,0},{1,17},{17,1},{2,18},{18,2},{3,19},{19,3},{4,20},{20... | collective-permute-start | bytes 6291464 | tf_op jit(solution)/shard_map/ppermute | solution.py:22
  484.7 179.7 %collective-permute-start.35 = (bf16[512,2048]{1,0:T(8,128)(2,1)}, bf16[512,2048]{1,0:T(8,128)(2,1)}, u32[]{:S(2)}, u32[]{:S(2)}) collective-permute-start(bf16[512,2048]{1,0:T(8,128)(2,1)} %convolution_convert_fusion.2), channel_id=1, source_target_pairs={{0,16},{16,0},{1,17},{17,1},{2,18},{18,2},{3,19},{19,3},{4,20},{20... | collective-permute-start | bytes 6291464 | tf_op jit(solution)/shard_map/ppermute | solution.py:22
  486.1 27.4 %collective-permute-start.64 = (bf16[2,128,1184]{1,2,0:T(8,128)(2,1)}, bf16[2,128,1184]{1,2,0:T(8,128)(2,1)}, u32[]{:S(2)}, u32[]{:S(2)}) collective-permute-start(bf16[2,128,1184]{1,2,0:T(8,128)(2,1)} %bitcast.470), channel_id=1, source_target_pairs={{0,2},{1,3},{2,0},{3,1},{4,6},{5,7},{6,4},{7,5},{8,10},{9,11},{10,... | collective-permute-start | bytes 1818632 | tf_op jit(solution)/shard_map/ppermute | solution.py:27
  497.6 15.0 %collective-permute-start.62 = (bf16[2,128,1152]{1,2,0:T(8,128)(2,1)S(1)}, bf16[2,128,1152]{1,2,0:T(8,128)(2,1)S(1)}, u32[]{:S(2)}, u32[]{:S(2)}) collective-permute-start(bf16[2,128,1152]{1,2,0:T(8,128)(2,1)S(1)} %select_bitcast_fusion.12), channel_id=1, source_target_pairs={{0,1},{1,0},{2,3},{3,2},{4,5},{5,4},{6,7},{7,6},{8,9},{9,8},{10,11... | collective-permute-start | bytes 1769480 | tf_op jit(solution)/shard_map/ppermute | solution.py:27
  505.9 57.1 %collective-permute-start.56 = (bf16[2,256,1024]{2,1,0:T(8,128)(2,1)}, bf16[2,256,1024]{2,1,0:T(8,128)(2,1)}, u32[]{:S(2)}, u32[]{:S(2)}) collective-permute-start(bf16[2,256,1024]{2,1,0:T(8,128)(2,1)} %bitcast.102), channel_id=1, source_target_pairs={{0,2},{1,3},{2,0},{3,1},{4,6},{5,7},{6,4},{7,5},{8,10},{9,11},{10,... | collective-permute-start | bytes 3145736 | tf_op jit(solution)/shard_map/ppermute | solution.py:27
  512.7 58.3 %collective-permute-start.54 = (bf16[2,128,2048]{2,1,0:T(8,128)(2,1)}, bf16[2,128,2048]{2,1,0:T(8,128)(2,1)}, u32[]{:S(2)}, u32[]{:S(2)}) collective-permute-start(bf16[2,128,2048]{2,1,0:T(8,128)(2,1)} %select_bitcast_fusion.4), channel_id=1, source_target_pairs={{0,1},{1,0},{2,3},{3,2},{4,5},{5,4},{6,7},{7,6},{8,9},{9,8},{10,11... | collective-permute-start | bytes 3145736 | tf_op jit(solution)/shard_map/ppermute | solution.py:27
  513.5 23.6 %collective-permute-start.63 = (bf16[128,1152]{0,1:T(8,128)(2,1)S(1)}, bf16[128,1152]{0,1:T(8,128)(2,1)S(1)}, u32[]{:S(2)}, u32[]{:S(2)}) collective-permute-start(bf16[128,1152]{0,1:T(8,128)(2,1)S(1)} %select_bitcast_fusion.38), channel_id=1, source_target_pairs={{0,2},{1,3},{2,0},{3,1},{4,6},{5,7},{6,4},{7,5},{8,10},{9,11},{10,... | collective-permute-start | bytes 884744 | tf_op jit(solution)/shard_map/ppermute | solution.py:27
  545.0 14.8 %collective-permute-start.31 = (bf16[128,2048]{1,0:T(8,128)(2,1)}, bf16[128,2048]{1,0:T(8,128)(2,1)}, u32[]{:S(2)}, u32[]{:S(2)}) collective-permute-start(bf16[128,2048]{1,0:T(8,128)(2,1)} %add_convert_fusion.9), channel_id=1, source_target_pairs={{4,0},{8,4},{12,8},{5,1},{9,5},{13,9},{6,2},{10,6},{14,10},{7,3},{... | collective-permute-start | bytes 1572872 | tf_op jit(solution)/shard_map/ppermute | solution.py:18
  563.0 31.2 %collective-permute-start.32 = (bf16[128,2048]{1,0:T(8,128)(2,1)S(1)}, bf16[128,2048]{1,0:T(8,128)(2,1)S(1)}, u32[]{:S(2)}, u32[]{:S(2)}) collective-permute-start(bf16[128,2048]{1,0:T(8,128)(2,1)S(1)} %add_convert_fusion.8), channel_id=1, source_target_pairs={{4,0},{8,4},{12,8},{5,1},{9,5},{13,9},{6,2},{10,6},{14,10},{7,3},{... | collective-permute-start | bytes 1572872 | tf_op jit(solution)/shard_map/ppermute | solution.py:18
  569.3 31.2 %collective-permute-start.57 = (bf16[256,1024]{1,0:T(8,128)(2,1)S(1)}, bf16[256,1024]{1,0:T(8,128)(2,1)S(1)}, u32[]{:S(2)}, u32[]{:S(2)}) collective-permute-start(bf16[256,1024]{1,0:T(8,128)(2,1)S(1)} %select_bitcast_fusion.19), channel_id=1, source_target_pairs={{0,1},{1,0},{2,3},{3,2},{4,5},{5,4},{6,7},{7,6},{8,9},{9,8},{10,11... | collective-permute-start | bytes 1572872 | tf_op jit(solution)/shard_map/ppermute | solution.py:27
  592.5 15.3 %collective-permute-start.55 = (bf16[128,2048]{1,0:T(8,128)(2,1)S(1)}, bf16[128,2048]{1,0:T(8,128)(2,1)S(1)}, u32[]{:S(2)}, u32[]{:S(2)}) collective-permute-start(bf16[128,2048]{1,0:T(8,128)(2,1)S(1)} %select_bitcast_fusion.20), channel_id=1, source_target_pairs={{0,2},{1,3},{2,0},{3,1},{4,6},{5,7},{6,4},{7,5},{8,10},{9,11},{10,... | collective-permute-start | bytes 1572872 | tf_op jit(solution)/shard_map/ppermute | solution.py:27
  594.2 46.7 %collective-permute-start.69 = (bf16[2,32,2336]{2,1,0:T(8,128)(2,1)}, bf16[2,32,2336]{2,1,0:T(8,128)(2,1)}, u32[]{:S(2)}, u32[]{:S(2)}) collective-permute-start(bf16[2,32,2336]{2,1,0:T(8,128)(2,1)} %pad_maximum_fusion.27), channel_id=1, source_target_pairs={{0,4},{4,0},{8,12},{12,8},{1,5},{5,1},{9,13},{13,9},{2,6},{6,2},{1... | collective-permute-start | bytes 897032 | tf_op jit(solution)/shard_map/ppermute | solution.py:27
  610.0 52.0 %collective-permute-start.58 = (bf16[2,32,4096]{2,1,0:T(8,128)(2,1)}, bf16[2,32,4096]{2,1,0:T(8,128)(2,1)}, u32[]{:S(2)}, u32[]{:S(2)}) collective-permute-start(bf16[2,32,4096]{2,1,0:T(8,128)(2,1)} %select_bitcast_fusion.18), channel_id=1, source_target_pairs={{0,4},{4,0},{8,12},{12,8},{1,5},{5,1},{9,13},{13,9},{2,6},{6,2},{1... | collective-permute-start | bytes 1572872 | tf_op jit(solution)/shard_map/ppermute | solution.py:27
  640.8 179.9 %collective-permute-start.34 = (bf16[256,1024]{1,0:T(8,128)(2,1)}, bf16[256,1024]{1,0:T(8,128)(2,1)}, u32[]{:S(2)}, u32[]{:S(2)}) collective-permute-start(bf16[256,1024]{1,0:T(8,128)(2,1)} %get-tuple-element.128), channel_id=1, source_target_pairs={{0,16},{16,0},{1,17},{17,1},{2,18},{18,2},{3,19},{19,3},{4,20},{20... | collective-permute-start | bytes 1572872 | tf_op jit(solution)/shard_map/ppermute | solution.py:22
  651.3 74.6 %collective-permute-start.45 = (bf16[512,2336]{0,1:T(8,128)(2,1)}, bf16[512,2336]{0,1:T(8,128)(2,1)}, u32[]{:S(2)}, u32[]{:S(2)}) collective-permute-start(bf16[512,2336]{0,1:T(8,128)(2,1)} %convolution_convert_fusion), channel_id=1, source_target_pairs={{0,16},{16,0},{1,17},{17,1},{2,18},{18,2},{3,19},{19,3},{4,20},{20... | collective-permute-start | bytes 7176200 | tf_op jit(solution)/shard_map/ppermute | solution.py:22
  660.7 32.0 %collective-permute-start.39 = (bf16[2,256,1024]{2,1,0:T(8,128)(2,1)S(1)}, bf16[2,256,1024]{2,1,0:T(8,128)(2,1)S(1)}, u32[]{:S(2)}, u32[]{:S(2)}) collective-permute-start(bf16[2,256,1024]{2,1,0:T(8,128)(2,1)S(1)} %bitcast.503), channel_id=1, source_target_pairs={{0,2},{1,3},{2,0},{3,1},{4,6},{5,7},{6,4},{7,5},{8,10},{9,11},{10,... | collective-permute-start | bytes 3145736 | tf_op jit(solution)/shard_map/ppermute | solution.py:27
  663.3 15.0 %collective-permute-start.59 = (bf16[32,4096]{1,0:T(8,128)(2,1)S(1)}, bf16[32,4096]{1,0:T(8,128)(2,1)S(1)}, u32[]{:S(2)}, u32[]{:S(2)}) collective-permute-start(bf16[32,4096]{1,0:T(8,128)(2,1)S(1)} %select_bitcast_fusion.42), channel_id=1, source_target_pairs={{0,8},{4,12},{8,0},{12,4},{1,9},{5,13},{9,1},{13,5},{2,10},{6,14},... | collective-permute-start | bytes 786440 | tf_op jit(solution)/shard_map/ppermute | solution.py:27
  678.6 26.1 %collective-permute-start.36 = (bf16[2,128,2048]{2,1,0:T(8,128)(2,1)S(1)}, bf16[2,128,2048]{2,1,0:T(8,128)(2,1)S(1)}, u32[]{:S(2)}, u32[]{:S(2)}) collective-permute-start(bf16[2,128,2048]{2,1,0:T(8,128)(2,1)S(1)} %select_bitcast_fusion.5), channel_id=1, source_target_pairs={{0,1},{1,0},{2,3},{3,2},{4,5},{5,4},{6,7},{7,6},{8,9},{9,8},{10,11... | collective-permute-start | bytes 3145736 | tf_op jit(solution)/shard_map/ppermute | solution.py:27
  692.7 14.9 %collective-permute-start.61 = (bf16[2,32,4096]{2,1,0:T(8,128)(2,1)S(1)}, bf16[2,32,4096]{2,1,0:T(8,128)(2,1)S(1)}, u32[]{:S(2)}, u32[]{:S(2)}) collective-permute-start(bf16[2,32,4096]{2,1,0:T(8,128)(2,1)S(1)} %pad_maximum_fusion.23), channel_id=1, source_target_pairs={{0,4},{4,0},{8,12},{12,8},{1,5},{5,1},{9,13},{13,9},{2,6},{6,2},{1... | collective-permute-start | bytes 1572872 | tf_op jit(solution)/shard_map/ppermute | solution.py:27
  694.0 23.4 %collective-permute-start.40 = (bf16[256,1024]{1,0:T(8,128)(2,1)}, bf16[256,1024]{1,0:T(8,128)(2,1)}, u32[]{:S(2)}, u32[]{:S(2)}) collective-permute-start(bf16[256,1024]{1,0:T(8,128)(2,1)} %select_bitcast_fusion.23), channel_id=1, source_target_pairs={{0,1},{1,0},{2,3},{3,2},{4,5},{5,4},{6,7},{7,6},{8,9},{9,8},{10,11... | collective-permute-start | bytes 1572872 | tf_op jit(solution)/shard_map/ppermute | solution.py:27
  706.3 14.9 %collective-permute-start.37 = (bf16[128,2048]{1,0:T(8,128)(2,1)}, bf16[128,2048]{1,0:T(8,128)(2,1)}, u32[]{:S(2)}, u32[]{:S(2)}) collective-permute-start(bf16[128,2048]{1,0:T(8,128)(2,1)} %select_bitcast_fusion.24), channel_id=1, source_target_pairs={{0,2},{1,3},{2,0},{3,1},{4,6},{5,7},{6,4},{7,5},{8,10},{9,11},{10,... | collective-permute-start | bytes 1572872 | tf_op jit(solution)/shard_map/ppermute | solution.py:27
  712.5 110.4 %collective-permute-start.71 = (bf16[128,4384]{0,1:T(8,128)(2,1)}, bf16[128,4384]{0,1:T(8,128)(2,1)}, u32[]{:S(2)}, u32[]{:S(2)}) collective-permute-start(bf16[128,4384]{0,1:T(8,128)(2,1)} %copy.343), channel_id=1, source_target_pairs={{0,16},{1,17},{2,18},{3,19},{4,20},{5,21},{6,22},{7,23},{8,24},{9,... | collective-permute-start | bytes 3366920 | tf_op jit(solution)/shard_map/ppermute | solution.py:414
  717.4 107.9 %collective-permute-start.73 = (bf16[256,1024]{1,0:T(8,128)(2,1)}, bf16[256,1024]{1,0:T(8,128)(2,1)}, u32[]{:S(2)}, u32[]{:S(2)}) collective-permute-start(bf16[256,1024]{1,0:T(8,128)(2,1)} %pad_maximum_fusion.25), channel_id=1, source_target_pairs={{0,16},{1,17},{2,18},{3,19},{4,20},{5,21},{6,22},{7,23},{8,24},{9,... | collective-permute-start | bytes 1572872 | tf_op jit(solution)/shard_map/ppermute | solution.py:414
  730.5 30.9 %collective-permute-start.48 = (bf16[2,128,1184]{1,2,0:T(8,128)(2,1)}, bf16[2,128,1184]{1,2,0:T(8,128)(2,1)}, u32[]{:S(2)}, u32[]{:S(2)}) collective-permute-start(bf16[2,128,1184]{1,2,0:T(8,128)(2,1)} %bitcast.471), channel_id=1, source_target_pairs={{0,2},{1,3},{2,0},{3,1},{4,6},{5,7},{6,4},{7,5},{8,10},{9,11},{10,... | collective-permute-start | bytes 1818632 | tf_op jit(solution)/shard_map/ppermute | solution.py:27
  761.2 15.6 %collective-permute-start.43 = (bf16[32,4096]{1,0:T(8,128)(2,1)S(1)}, bf16[32,4096]{1,0:T(8,128)(2,1)}, u32[]{:S(2)}, u32[]{:S(2)}) collective-permute-start(bf16[32,4096]{1,0:T(8,128)(2,1)S(1)} %fusion.103), channel_id=1, source_target_pairs={{0,8},{4,12},{8,0},{12,4},{1,9},{5,13},{9,1},{13,5},{2,10},{6,14},... | collective-permute-start | bytes 786440 | tf_op jit(solution)/shard_map/ppermute | solution.py:27
  789.8 15.2 %collective-permute-start.44 = (bf16[2,32,4096]{2,1,0:T(8,128)(2,1)S(1)}, bf16[2,32,4096]{2,1,0:T(8,128)(2,1)S(1)}, u32[]{:S(2)}, u32[]{:S(2)}) collective-permute-start(bf16[2,32,4096]{2,1,0:T(8,128)(2,1)S(1)} %pad_maximum_fusion.22), channel_id=1, source_target_pairs={{0,4},{4,0},{8,12},{12,8},{1,5},{5,1},{9,13},{13,9},{2,6},{6,2},{1... | collective-permute-start | bytes 1572872 | tf_op jit(solution)/shard_map/ppermute | solution.py:27
  (278 other events, 1897.8 us)
Sparse Core Ops, SparseCore 0:
  73.3 36.0 all-gather.3
  111.2 55.9 all-gather.5
  208.3 32.6 all-gather.7
